TPU v7x, 256 devices: a whole 4x4x8 slice. The times are simulated.
256 devices in a mesh: seq: 64 (over x, z, core), sp: 4 (over y).
Axes of the slice: x: 4, y: 4, z: 8, core: 2. Of those that a mesh axis runs over, the one named last changes fastest.
Arguments:
- latents: bfloat16 [128, 32, 128], P('seq', None, 'sp'), may hold values from -6 to 6
- conv_in_weight: bfloat16 [432, 384], replicated, may hold values from -0.3125 to 0.3125
- norm_gain: float32 [384], replicated, may hold values from 0.25 to 1.75
- conv_weight: bfloat16 [10368, 384], P(None, 'sp'), may hold values from -0.0625 to 0.0625
- frame_list: int32 [64], replicated, may hold values from 0 to 127, as said below
- reward_scale: float32 [64], P('seq'), may hold values from 0.5 to 2
- patch_weight: bfloat16 [1536, 1024], replicated, may hold values from -0.15625 to 0.15625
- ln_gain: float32 [2, 1024], replicated, may hold values from 0.25 to 1.75
- qkv_weight: bfloat16 [1024, 3072], P(None, 'sp'), may hold values from -0.1875 to 0.1875
- out_weight: bfloat16 [1024, 1024], P('sp'), may hold values from -0.1875 to 0.1875
- head_vec: float32 [1024], replicated, may hold values from -1.5 to 1.5
Outputs:
- rewards: float32 [64], P('seq')
- latent_grad: float32 [128, 32, 128], P('seq', None, 'sp')
Inputs may be any that keep to these rules, and one draw needn't show every extreme that they name: `frame_list`: entry j is a frame of clip j // 8, that is between (j // 8) * 16 and that plus 16 - 1; within a clip the entries are distinct and rising.
All inputs are finite; a program needn't handle non-finite values.
Results may differ from a plain program's by a relative error of at most 0.038.
Values may be sent and summed in bfloat16 or wider, within the bound.
A program may use at most 128 MiB of HBM per device.

v0:
```python
import jax
import jax.numpy as jnp
from jax import lax
from jax.sharding import PartitionSpec as P

LAT = 16
CH = 384
HD = 64
FR_DEV = 2
ROWS = 8
COLS = 8
CLIP_FR = 16


norm_epsilon = 1e-06
layer_epsilon = 1e-05


def passed_along(value, axis, steps):
    count = lax.axis_size(axis)
    leading, last = (max(0, -steps), min(count, count - steps))
    return lax.ppermute(value, axis, [(source, source + steps) for source in range(leading, last)])


def with_halo(block, sides, width):
    for axis, dim in sides:
        count = lax.axis_size(axis)
        forward = [(i, i + 1) for i in range(count - 1)]
        backward = [(target, source) for source, target in forward]
        low = lax.ppermute(
            lax.slice_in_dim(block, block.shape[dim] - width, None, axis=dim), axis, forward
        )
        high = lax.ppermute(lax.slice_in_dim(block, 0, width, axis=dim), axis, backward)
        block = jnp.concatenate([low, block, high], axis=dim)
    return block


def gather_columns(padded, frames, height_in, width_in):
    windows = []
    for time_lag in range(3):
        for row_lag in range(3):
            for col_lag in range(3):
                windows.append(
                    padded[
                        time_lag : time_lag + frames,
                        row_lag : row_lag + height_in,
                        col_lag : col_lag + width_in,
                    ]
                )
    stacked = jnp.concatenate(windows, axis=-1)
    return stacked.reshape(frames * height_in * width_in, stacked.shape[-1])


def scatter_columns(columns, shape, frames, height_in, width_in):
    blank_ext = jnp.zeros(shape, jnp.float32)
    _, pullback = jax.vjp(
        lambda padded: gather_columns(padded, frames, height_in, width_in), blank_ext
    )
    return pullback(columns)[0]


def contract_last(left, right):
    return lax.dot_general(
        left, right, (((1,), (1,)), ((), ())), preferred_element_type=jnp.float32
    )


def activate(volume, scaling):
    inverse = lax.rsqrt(jnp.mean(volume * volume, axis=-1, keepdims=True) + norm_epsilon)
    return jax.nn.silu(volume * inverse * scaling)


def layer_norm(volume, scaling):
    center = jnp.mean(volume, axis=-1, keepdims=True)
    spread = jnp.mean((volume - center) ** 2, axis=-1, keepdims=True)
    return (volume - center) * lax.rsqrt(spread + layer_epsilon) * scaling


def layer_norm_back(volume, scaling, cotangent):
    center = jnp.mean(volume, axis=-1, keepdims=True)
    spread = jnp.mean((volume - center) ** 2, axis=-1, keepdims=True)
    inverse = lax.rsqrt(spread + layer_epsilon)
    whitened = (volume - center) * inverse
    scaled_grad = cotangent * scaling
    return inverse * (
        scaled_grad
        - jnp.mean(scaled_grad, axis=-1, keepdims=True)
        - whitened * jnp.mean(scaled_grad * whitened, axis=-1, keepdims=True)
    )


def patchify(picture):
    height_in, width_in, channels = picture.shape
    blocks = picture.reshape(height_in // 2, 2, width_in // 2, 2, channels).transpose(0, 2, 1, 3, 4)
    return blocks.reshape(height_in // 2 * (width_in // 2), 4 * channels)


def unpatchify(tokens_in, height_in, width_in, channels):
    blocks = tokens_in.reshape(height_in // 2, width_in // 2, 2, 2, channels).transpose(
        0, 2, 1, 3, 4
    )
    return blocks.reshape(height_in, width_in, channels)


def extend(volume, keep_past):
    earlier = passed_along(volume, "seq", 1) * keep_past
    joined = jnp.concatenate([earlier, volume], axis=0)
    rimmed = with_halo(joined, (("sp", 1),), 1)
    return jnp.pad(rimmed, ((0, 0), (0, 0), (1, 1), (0, 0)))


def retract(grad_padded, keep_past):
    inner_cols = grad_padded[:, :, 1:-1]
    from_below = passed_along(inner_cols[:, 0], "sp", -1)
    from_above = passed_along(inner_cols[:, -1], "sp", 1)
    middle = inner_cols[:, 1:-1]
    middle = middle.at[:, -1].add(from_below).at[:, 0].add(from_above)
    earlier = middle[:FR_DEV] * keep_past
    later_grad = passed_along(earlier.astype(jnp.bfloat16), "seq", -1).astype(earlier.dtype)
    return middle[FR_DEV:] + later_grad


def near_frames(flat_feats, frame_list, owner, seq_count, group_size):
    own_frames = owner * FR_DEV + jnp.arange(FR_DEV, dtype=jnp.int32)

    def outgoing(offset):
        target_index = jnp.clip(owner + offset, 0, seq_count - 1)
        frame_index = lax.dynamic_index_in_dim(frame_list, target_index, 0, keepdims=False)
        hit_rows = (own_frames == frame_index).astype(jnp.bfloat16)
        return jnp.dot(hit_rows, flat_feats, preferred_element_type=jnp.float32).astype(
            jnp.bfloat16
        )

    running_sum = outgoing(0).astype(jnp.float32)
    for offset in range(1 - group_size, group_size):
        if offset != 0:
            arrived = passed_along(outgoing(offset), "seq", offset)
            running_sum = running_sum + arrived.astype(jnp.float32)
    return running_sum.astype(jnp.bfloat16)


def near_grads(frame_grad, frame_list, owner, seq_count, group_size):
    own_frames = owner * FR_DEV + jnp.arange(FR_DEV, dtype=jnp.int32)

    def incoming(source_grad, offset):
        source_index = jnp.clip(owner + offset, 0, seq_count - 1)
        frame_index = lax.dynamic_index_in_dim(frame_list, source_index, 0, keepdims=False)
        hit_rows = (own_frames == frame_index).astype(jnp.float32)
        return hit_rows[:, None] * source_grad[None, :].astype(jnp.float32)

    running_sum = incoming(frame_grad, 0)
    for offset in range(1 - group_size, group_size):
        if offset != 0:
            arrived = passed_along(frame_grad, "seq", -offset)
            running_sum = running_sum + incoming(arrived, offset)
    return running_sum.astype(jnp.bfloat16)


def score_frame(picture, weighting, patch_weight, ln_gain, qkv_weight, out_weight, head_vec):
    scale_attn = HD ** (-0.5)
    patches = patchify(picture)
    tokens_x = jnp.dot(patches, patch_weight, preferred_element_type=jnp.float32).astype(
        jnp.bfloat16
    )
    own_tokens = tokens_x.shape[0]
    total_tokens = own_tokens * lax.axis_size("sp")
    normed_in = layer_norm(
        lax.all_gather(tokens_x, "sp", axis=0, tiled=True).astype(jnp.float32), ln_gain[0]
    ).astype(jnp.bfloat16)
    qkv = jnp.dot(normed_in, qkv_weight, preferred_element_type=jnp.float32).astype(jnp.bfloat16)
    local_heads = qkv.shape[1] // (3 * HD)
    qkv = qkv.reshape(total_tokens, local_heads, 3, HD)
    query, key_part, value_part = (qkv[:, :, 0], qkv[:, :, 1], qkv[:, :, 2])
    scores = (
        jnp.einsum("qhd,khd->hqk", query, key_part, preferred_element_type=jnp.float32) * scale_attn
    )
    attention = jax.nn.softmax(scores, axis=-1)
    attn_low = attention.astype(jnp.bfloat16)
    mixed = jnp.einsum(
        "hqk,khd->qhd", attn_low, value_part, preferred_element_type=jnp.float32
    ).astype(jnp.bfloat16)
    mixed = mixed.reshape(total_tokens, local_heads * HD)
    attn_sum = lax.psum_scatter(
        jnp.dot(mixed, out_weight, preferred_element_type=jnp.float32).astype(jnp.bfloat16),
        "sp",
        scatter_dimension=0,
        tiled=True,
    ).astype(jnp.float32)
    resid = tokens_x.astype(jnp.float32) + attn_sum
    normed_out = layer_norm(resid, ln_gain[1])
    reward = lax.psum(jnp.sum(normed_out * head_vec) / total_tokens, "sp")
    grad_norm = jnp.broadcast_to(weighting / total_tokens * head_vec, resid.shape)
    grad_resid = layer_norm_back(resid, ln_gain[1], grad_norm)
    grad_mixed = contract_last(
        lax.all_gather(grad_resid.astype(jnp.bfloat16), "sp", axis=0, tiled=True), out_weight
    ).astype(jnp.bfloat16)
    grad_mixed = grad_mixed.reshape(total_tokens, local_heads, HD)
    grad_attn = jnp.einsum(
        "qhd,khd->hqk", grad_mixed, value_part, preferred_element_type=jnp.float32
    )
    grad_scores = (
        attention
        * (grad_attn - jnp.sum(grad_attn * attention, axis=-1, keepdims=True))
        * scale_attn
    ).astype(jnp.bfloat16)
    grad_query = jnp.einsum(
        "hqk,khd->qhd", grad_scores, key_part, preferred_element_type=jnp.float32
    ).astype(jnp.bfloat16)
    grad_keyset = jnp.einsum(
        "hqk,qhd->khd", grad_scores, query, preferred_element_type=jnp.float32
    ).astype(jnp.bfloat16)
    grad_values = jnp.einsum(
        "hqk,qhd->khd", attn_low, grad_mixed, preferred_element_type=jnp.float32
    ).astype(jnp.bfloat16)
    grad_qkv = jnp.stack([grad_query, grad_keyset, grad_values], axis=2).reshape(
        total_tokens, local_heads * 3 * HD
    )
    grad_normed = lax.psum_scatter(
        contract_last(grad_qkv, qkv_weight).astype(jnp.bfloat16),
        "sp",
        scatter_dimension=0,
        tiled=True,
    ).astype(jnp.float32)
    grad_tokens = (
        grad_resid + layer_norm_back(tokens_x.astype(jnp.float32), ln_gain[0], grad_normed)
    ).astype(jnp.bfloat16)
    grad_patch = contract_last(grad_tokens, patch_weight).astype(jnp.bfloat16)
    return (reward, unpatchify(grad_patch, ROWS, COLS, CH).reshape(ROWS * COLS * CH))


def body(
    latents,
    conv_in_weight,
    norm_gain,
    conv_weight,
    frame_list,
    reward_scale,
    patch_weight,
    ln_gain,
    qkv_weight,
    out_weight,
    head_vec,
):
    seq_count = lax.axis_size("seq")
    owner = lax.axis_index("seq")
    group_size = CLIP_FR // FR_DEV
    keep_past = (owner * FR_DEV % CLIP_FR != 0).astype(jnp.bfloat16)
    keep_float = keep_past.astype(jnp.float32)
    cells = FR_DEV * ROWS * COLS
    planar = lax.all_to_all(latents, "sp", split_axis=1, concat_axis=2, tiled=True)
    volume = planar.reshape(FR_DEV, ROWS, COLS, LAT)
    padded_in = extend(volume, keep_past)
    first = jnp.dot(
        gather_columns(padded_in, FR_DEV, ROWS, COLS),
        conv_in_weight,
        preferred_element_type=jnp.float32,
    )
    first = first.reshape(FR_DEV, ROWS, COLS, CH).astype(jnp.bfloat16)
    first_f = first.astype(jnp.float32)
    active = activate(first_f, norm_gain).astype(jnp.bfloat16)
    whole_conv = lax.all_gather(conv_weight, "sp", axis=1, tiled=True)
    padded_mid = extend(active, keep_past)
    block_out = jnp.dot(
        gather_columns(padded_mid, FR_DEV, ROWS, COLS),
        whole_conv,
        preferred_element_type=jnp.float32,
    )
    feats = (first_f + block_out.reshape(FR_DEV, ROWS, COLS, CH)).astype(jnp.bfloat16)
    flat_feats = feats.reshape(FR_DEV, ROWS * COLS * CH)
    picked = near_frames(flat_feats, frame_list, owner, seq_count, group_size)
    reward, frame_grad = score_frame(
        picked.reshape(ROWS, COLS, CH),
        reward_scale[0],
        patch_weight,
        ln_gain,
        qkv_weight,
        out_weight,
        head_vec,
    )
    grad_feats = near_grads(frame_grad, frame_list, owner, seq_count, group_size)
    grad_feats = grad_feats.reshape(FR_DEV, ROWS, COLS, CH)
    grad_columns = contract_last(grad_feats.reshape(cells, CH), whole_conv)
    grad_padded = scatter_columns(grad_columns, padded_mid.shape, FR_DEV, ROWS, COLS)
    grad_active = retract(grad_padded, keep_float)
    _, pullback = jax.vjp(lambda volume_in: activate(volume_in, norm_gain), first_f)
    grad_first = (grad_feats.astype(jnp.float32) + pullback(grad_active)[0]).astype(jnp.bfloat16)
    grad_in_columns = contract_last(grad_first.reshape(cells, CH), conv_in_weight)
    grad_in_padded = scatter_columns(grad_in_columns, padded_in.shape, FR_DEV, ROWS, COLS)
    grad_latent = retract(grad_in_padded, keep_float).reshape(FR_DEV, ROWS, COLS * LAT)
    latent_grad = lax.all_to_all(grad_latent, "sp", split_axis=2, concat_axis=1, tiled=True)
    return (reward[None], latent_grad)


def solution(mesh):
    in_specs = (
        P("seq", None, "sp"),
        P(),
        P(),
        P(None, "sp"),
        P(),
        P("seq"),
        P(),
        P(),
        P(None, "sp"),
        P("sp", None),
        P(),
    )
    out_specs = (P("seq"), P("seq", None, "sp"))
    return jax.shard_map(body, mesh=mesh, in_specs=in_specs, out_specs=out_specs, check_vma=False)
```

profile of v0, /device:TPU:2, one launch (start us, length us, event | category | flops | bytes accessed | tf_op | source)
XLA Modules:
  0.0 418.2 jit_solution(15405841624743117908)
XLA Ops:
  9.5 4.5 %all-to-all-start = ((bf16[4,2,256]{2,1,0:T(2,128)(2,1)}), bf16[4,2,256]{2,1,0:T(2,128)(2,1)S(1)}, u32[]{:S(2)}, u32[]{:S(2)}) async-start(bf16[4,2,256]{2,1,0:T(2,128)(2,1)} %reshape.748), calls=%async_computation | async-start | bytes 8192 | tf_op jit(solution)/shard_map/all_to_all | solution.py:250
  16.0 1.8 fusion.183
  17.9 1.9 fusion.193
  20.0 1.9 collective-permute-start
  21.9 1.8 compare_convert_fusion
  23.7 4.7 %collective-permute-done = bf16[2,8,8,16]{3,2,1,0:T(8,128)(2,1)S(1)} collective-permute-done((bf16[2,8,8,16]{3,2,1,0:T(8,128)(2,1)S(1)}, bf16[2,8,8,16]{3,2,1,0:T(8,128)(2,1)S(1)}, u32[]{:S(2)}, u32[]{:S(2)}) %collective-permute-start) | collective-permute-done | bytes 4128 | tf_op jit(solution)/shard_map/ppermute | solution.py:22
  29.8 4.5 %collective-permute-start.1 = (bf16[4,1,8,16]{3,2,1,0:T(8,128)(2,1)S(1)}, bf16[4,1,8,16]{3,2,1,0:T(8,128)(2,1)S(1)}, u32[]{:S(2)}, u32[]{:S(2)}) collective-permute-start(bf16[4,1,8,16]{3,2,1,0:T(8,128)(2,1)S(1)} %get-tuple-element.150), channel_id=1, source_target_pairs={{0,1},{1,2},{2,3},{4,5},{5,6},{6,7},{8,9},{9,10},{10,11},{12,13},{... | collective-permute-start | bytes 3080 | tf_op jit(solution)/shard_map/ppermute | solution.py:30
  41.0 1.9 collective-permute-start.3
  42.9 1.8 compare_convert_fusion.2
  44.8 4.3 %collective-permute-done.3 = bf16[2,8,8,384]{3,2,1,0:T(8,128)(2,1)S(1)} collective-permute-done((bf16[2,8,8,384]{3,2,1,0:T(8,128)(2,1)S(1)}, bf16[2,8,8,384]{3,2,1,0:T(8,128)(2,1)S(1)}, u32[]{:S(2)}, u32[]{:S(2)}) %collective-permute-start.3) | collective-permute-done | bytes 98336 | tf_op jit(solution)/shard_map/ppermute | solution.py:22
  50.4 4.9 %collective-permute-start.4 = (bf16[4,1,8,384]{3,2,1,0:T(8,128)(2,1)S(1)}, bf16[4,1,8,384]{3,2,1,0:T(8,128)(2,1)S(1)}, u32[]{:S(2)}, u32[]{:S(2)}) collective-permute-start(bf16[4,1,8,384]{3,2,1,0:T(8,128)(2,1)S(1)} %get-tuple-element.122), channel_id=1, source_target_pairs={{0,1},{1,2},{2,3},{4,5},{5,6},{6,7},{8,9},{9,10},{10,11},{12,13},{... | collective-permute-start | bytes 73736 | tf_op jit(solution)/shard_map/ppermute | solution.py:30
  55.3 1.9 compare_convert_fusion.4
  75.9 19.6 %all-gather.2.cloned.1.call-done = bf16[10368,384]{0,1:T(8,128)(2,1)} async-done(((bf16[10368,96]{0,1:T(8,128)(2,1)}), bf16[10368,384]{0,1:T(8,128)(2,1)}) %all-gather.2.cloned.1.call-update) | async-done | bytes 7962640 | tf_op jit(solution)/shard_map/all_gather | solution.py:261
  95.6 6.5 %fusion.18 = bf16[1,2,64,384]{3,2,1,0:T(8,128)(2,1)S(1)} fusion(f32[2,8,8,384]{3,2,1,0:T(8,128)S(1)} %get-tuple-element.172, bf16[2,8,8,10368]{3,2,1,0:T(8,128)(2,1)} %slice_dynamic-update-slice_fusion, bf16[10368,384]{0,1:T(8,128)(2,1)} %all-gather.2.cloned.1.call-done), kind=kOutput, calls=%fused_computation.22 | convolution fusion | flops 1019314176 | bytes 10911744 | tf_op jit(solution)/shard_map/dot_general | solution.py:263
  107.5 4.9 %collective-permute-start.19 = (bf16[24576]{0:T(1024)(128)(2,1)S(1)}, bf16[24576]{0:T(1024)(128)(2,1)S(1)}, u32[]{:S(2)}, u32[]{:S(2)}) collective-permute-start(bf16[24576]{0:T(1024)(128)(2,1)S(1)} %convert_element_type.401), channel_id=1, source_target_pairs={{0,28},{4,32},{8,36},{12,40},{16,44},{20,48},{24,52},{28,56},{32,6... | collective-permute-start | bytes 147464 | tf_op jit(solution)/shard_map/ppermute | solution.py:22
  112.4 4.9 %collective-permute-start.18 = (bf16[24576]{0:T(1024)(128)(2,1)S(1)}, bf16[24576]{0:T(1024)(128)(2,1)S(1)}, u32[]{:S(2)}, u32[]{:S(2)}) collective-permute-start(bf16[24576]{0:T(1024)(128)(2,1)S(1)} %convert_element_type.399), channel_id=1, source_target_pairs={{0,24},{4,28},{8,32},{12,36},{16,40},{20,44},{24,48},{28,52},{32,5... | collective-permute-start | bytes 147464 | tf_op jit(solution)/shard_map/ppermute | solution.py:22
  117.3 3.8 collective-permute-start.17
  121.1 4.4 %collective-permute-start.16 = (bf16[24576]{0:T(1024)(128)(2,1)S(1)}, bf16[24576]{0:T(1024)(128)(2,1)S(1)}, u32[]{:S(2)}, u32[]{:S(2)}) collective-permute-start(bf16[24576]{0:T(1024)(128)(2,1)S(1)} %convert_element_type.395), channel_id=1, source_target_pairs={{0,16},{4,20},{8,24},{12,28},{16,32},{20,36},{24,40},{28,44},{32,4... | collective-permute-start | bytes 147464 | tf_op jit(solution)/shard_map/ppermute | solution.py:22
  125.6 4.1 collective-permute-start.15
  135.8 2.6 collective-permute-start.14
  138.4 2.4 collective-permute-start.13
  140.8 5.3 %collective-permute-start.12 = (bf16[24576]{0:T(1024)(128)(2,1)S(1)}, bf16[24576]{0:T(1024)(128)(2,1)S(1)}, u32[]{:S(2)}, u32[]{:S(2)}) collective-permute-start(bf16[24576]{0:T(1024)(128)(2,1)S(1)} %convert_element_type.387), channel_id=1, source_target_pairs={{4,0},{8,4},{12,8},{16,12},{20,16},{24,20},{28,24},{32,28},{36,32}... | collective-permute-start | bytes 147464 | tf_op jit(solution)/shard_map/ppermute | solution.py:22
  146.1 3.3 collective-permute-start.11
  150.4 1.9 collective-permute-start.10
  152.4 2.1 collective-permute-start.9
  154.5 3.9 collective-permute-start.8
  158.4 1.9 collective-permute-start.7
  160.4 1.9 collective-permute-start.6
  163.2 3.6 collective-permute-done.7
  166.8 2.5 collective-permute-done.6
  170.1 12.2 %all_gather.10 = bf16[64,1024]{1,0:T(8,128)(2,1)S(1)} all-gather(bf16[16,1024]{1,0:T(8,128)(2,1)S(1)} %convolution_convert_fusion.10), channel_id=1, replica_groups=mesh['seq'=64,'sp'=4] {'sp'}, dimensions={0}, use_global_device_ids=true | all-gather | bytes 163840 | tf_op jit(solution)/shard_map/all_gather | solution.py:168
  184.0 2.2 fusion.188
  186.9 1.8 fusion.194
  189.9 1.9 convolution_convert_fusion.1
  191.9 1.8 compare_convert_fusion.6
  195.0 20.4 %reduce-scatter.3.cloned.1.call-done = bf16[16,1024]{1,0:T(8,128)(2,1)} async-done(((bf16[64,1024]{1,0:T(8,128)(2,1)}), bf16[16,1024]{1,0:T(8,128)(2,1)}) %reduce-scatter.3.cloned.1.call-update) | async-done | bytes 32784 | tf_op jit(solution)/shard_map/reduce_scatter | solution.py:183
  219.8 12.2 %all_gather.11 = bf16[64,1024]{1,0:T(8,128)(2,1)S(1)} all-gather(bf16[16,1024]{1,0:T(8,128)(2,1)S(1)} %fusion.80), channel_id=1, replica_groups=mesh['seq'=64,'sp'=4] {'sp'}, dimensions={0}, use_global_device_ids=true | all-gather | bytes 163840 | tf_op jit(solution)/shard_map/all_gather | solution.py:195
  240.4 1.9 copy.223
  243.4 2.7 convolution_convert_fusion.2
  246.1 1.8 compare_convert_fusion.8
  247.8 21.1 %reduce-scatter.5.cloned.1.call-done = bf16[16,1024]{1,0:T(8,128)(2,1)} async-done(((bf16[64,1024]{1,0:T(8,128)(2,1)}), bf16[16,1024]{1,0:T(8,128)(2,1)}) %reduce-scatter.5.cloned.1.call-update) | async-done | bytes 32784 | tf_op jit(solution)/shard_map/reduce_scatter | solution.py:218
  272.4 4.9 %collective-permute-start.33 = (bf16[24576]{0:T(1024)(128)(2,1)}, bf16[24576]{0:T(1024)(128)(2,1)S(1)}, u32[]{:S(2)}, u32[]{:S(2)}) collective-permute-start(bf16[24576]{0:T(1024)(128)(2,1)} %reshape_reshape.8), channel_id=1, source_target_pairs={{28,0},{32,4},{36,8},{40,12},{44,16},{48,20},{52,24},{56,28},{60,3... | collective-permute-start | bytes 147464 | tf_op jit(solution)/shard_map/ppermute | solution.py:22
  277.2 3.9 collective-permute-start.32
  281.1 2.8 collective-permute-start.31
  283.9 2.3 collective-permute-start.30
  287.9 1.9 collective-permute-start.29
  289.9 2.2 collective-permute-start.28
  292.1 2.0 collective-permute-start.27
  294.1 2.3 collective-permute-start.26
  296.5 3.7 collective-permute-start.25
  300.1 1.8 compare_convert_fusion.12
  302.0 4.3 %collective-permute-start.24 = (bf16[24576]{0:T(1024)(128)(2,1)}, bf16[24576]{0:T(1024)(128)(2,1)}, u32[]{:S(2)}, u32[]{:S(2)}) collective-permute-start(bf16[24576]{0:T(1024)(128)(2,1)} %reshape_reshape.8), channel_id=1, source_target_pairs={{0,12},{4,16},{8,20},{12,24},{16,28},{20,32},{24,36},{28,40},{32,4... | collective-permute-start | bytes 147464 | tf_op jit(solution)/shard_map/ppermute | solution.py:22
  306.3 5.7 %collective-permute-start.23 = (bf16[24576]{0:T(1024)(128)(2,1)}, bf16[24576]{0:T(1024)(128)(2,1)}, u32[]{:S(2)}, u32[]{:S(2)}) collective-permute-start(bf16[24576]{0:T(1024)(128)(2,1)} %reshape_reshape.8), channel_id=1, source_target_pairs={{0,16},{4,20},{8,24},{12,28},{16,32},{20,36},{24,40},{28,44},{32,4... | collective-permute-start | bytes 147464 | tf_op jit(solution)/shard_map/ppermute | solution.py:22
  312.0 4.0 collective-permute-start.22
  316.1 7.4 %collective-permute-start.21 = (bf16[24576]{0:T(1024)(128)(2,1)}, bf16[24576]{0:T(1024)(128)(2,1)}, u32[]{:S(2)}, u32[]{:S(2)}) collective-permute-start(bf16[24576]{0:T(1024)(128)(2,1)} %reshape_reshape.8), channel_id=1, source_target_pairs={{0,24},{4,28},{8,32},{12,36},{16,40},{20,44},{24,48},{28,52},{32,5... | collective-permute-start | bytes 147464 | tf_op jit(solution)/shard_map/ppermute | solution.py:22
  323.5 3.7 collective-permute-start.20
  350.9 4.8 %fusion.4 = f32[2,8,8,10368]{3,2,0,1:T(8,128)S(1)} fusion(bf16[10368,384]{0,1:T(8,128)(2,1)} %all-gather.2.cloned.1.call-done, bf16[2,8,8,384]{3,2,1,0:T(8,128)(2,1)S(1)} %add_convert_fusion), kind=kOutput, calls=%fused_computation.4 | convolution fusion | flops 1019215872 | bytes 13369344 | tf_op jit(solution)/shard_map/dot_general | solution.py:63
  361.8 4.5 %collective-permute-start.35 = (f32[4,8,384]{2,1,0:T(8,128)S(1)}, f32[4,8,384]{2,1,0:T(8,128)S(1)}, u32[]{:S(2)}, u32[]{:S(2)}) collective-permute-start(f32[4,8,384]{2,1,0:T(8,128)S(1)} %get-tuple-element.86), channel_id=1, source_target_pairs={{0,1},{1,2},{2,3},{4,5},{5,6},{6,7},{8,9},{9,10},{10,11},{12,13},{... | collective-permute-start | bytes 147464 | tf_op jit(solution)/shard_map/ppermute | solution.py:22
  368.1 4.3 %collective-permute-start.36 = (bf16[2,8,8,384]{3,2,1,0:T(8,128)(2,1)S(1)}, bf16[2,8,8,384]{3,2,1,0:T(8,128)(2,1)S(1)}, u32[]{:S(2)}, u32[]{:S(2)}) collective-permute-start(bf16[2,8,8,384]{3,2,1,0:T(8,128)(2,1)S(1)} %fusion.47), channel_id=1, source_target_pairs={{4,0},{8,4},{12,8},{16,12},{20,16},{24,20},{28,24},{32,28},{36,32}... | collective-permute-start | bytes 294920 | tf_op jit(solution)/shard_map/ppermute | solution.py:22
  372.4 2.2 collective-permute-done.36
  378.1 4.6 %collective-permute-start.38 = (f32[4,8,16]{2,1,0:T(8,128)S(1)}, f32[4,8,16]{2,1,0:T(8,128)S(1)}, u32[]{:S(2)}, u32[]{:S(2)}) collective-permute-start(f32[4,8,16]{2,1,0:T(8,128)S(1)} %get-tuple-element.88), channel_id=1, source_target_pairs={{0,1},{1,2},{2,3},{4,5},{5,6},{6,7},{8,9},{9,10},{10,11},{12,13},{... | collective-permute-start | bytes 6152 | tf_op jit(solution)/shard_map/ppermute | solution.py:22
  384.1 5.0 %collective-permute-start.39 = (bf16[2,8,8,16]{3,2,0,1:T(8,128)(2,1)S(1)}, bf16[2,8,8,16]{3,2,0,1:T(8,128)(2,1)S(1)}, u32[]{:S(2)}, u32[]{:S(2)}) collective-permute-start(bf16[2,8,8,16]{3,2,0,1:T(8,128)(2,1)S(1)} %fusion.70), channel_id=1, source_target_pairs={{4,0},{8,4},{12,8},{16,12},{20,16},{24,20},{28,24},{32,28},{36,32}... | collective-permute-start | bytes 12296 | tf_op jit(solution)/shard_map/ppermute | solution.py:22
  391.7 5.0 %all-to-all-start.1 = ((f32[4,1,512]{2,1,0:T(1,128)}), f32[4,1,512]{2,1,0:T(1,128)S(1)}, u32[]{:S(2)}, u32[]{:S(2)}) async-start(f32[4,1,512]{2,1,0:T(1,128)} %reshape.750), calls=%async_computation.3 | async-start | bytes 16384 | tf_op jit(solution)/shard_map/all_to_all | solution.py:290
  397.4 12.1 %psum.7 = f32[1]{0:T(128)} all-reduce(f32[1]{0:T(128)} %bitcast.59), channel_id=1, replica_groups=mesh['seq'=64,'sp'=4] {'sp'}, use_global_device_ids=true, to_apply=%region_9.10 | all-reduce | flops 1 | bytes 8 | tf_op jit(solution)/shard_map/psum | solution.py:191
  (263 shorter events, 110.0 us)
Async XLA Ops:
  7.2 162.4 %copy-start = (bf16[1536,1024]{1,0:T(8,128)(2,1)S(1)}, bf16[1536,1024]{1,0:T(8,128)(2,1)}, u32[]{:S(2)}) copy-start(bf16[1536,1024]{1,0:T(8,128)(2,1)} %param.25) | copy-start | bytes 9437188
  7.2 88.4 %all-gather.2.cloned.1.call-start = ((), (), s32[]{:S(2)}) async-start(), calls=%async_computation.4 | async-start | bytes 9953280 | tf_op jit(solution)/shard_map/all_gather | solution.py:261
  9.5 10.3 %all-to-all-start = ((bf16[4,2,256]{2,1,0:T(2,128)(2,1)}), bf16[4,2,256]{2,1,0:T(2,128)(2,1)S(1)}, u32[]{:S(2)}, u32[]{:S(2)}) async-start(bf16[4,2,256]{2,1,0:T(2,128)(2,1)} %reshape.748), calls=%async_computation | async-start | bytes 8192 | tf_op jit(solution)/shard_map/all_to_all | solution.py:250
  14.0 201.4 %reduce-scatter.3.cloned.1.call-start = ((), (), s32[]{:S(2)}) async-start(), calls=%async_computation.5 | async-start | bytes 163840 | tf_op jit(solution)/shard_map/reduce_scatter | solution.py:183
  20.0 8.5 %collective-permute-start = (bf16[2,8,8,16]{3,2,1,0:T(8,128)(2,1)S(1)}, bf16[2,8,8,16]{3,2,1,0:T(8,128)(2,1)S(1)}, u32[]{:S(2)}, u32[]{:S(2)}) collective-permute-start(bf16[2,8,8,16]{3,2,1,0:T(8,128)(2,1)S(1)} %reshape.688), channel_id=1, source_target_pairs={{0,4},{4,8},{8,12},{12,16},{16,20},{20,24},{24,28},{28,32},{32,36}... | collective-permute-start | bytes 12296 | tf_op jit(solution)/shard_map/ppermute | solution.py:22
  28.5 5.9 %collective-permute-start.2 = (bf16[4,1,8,16]{3,2,1,0:T(8,128)(2,1)S(1)}, bf16[4,1,8,16]{3,2,1,0:T(8,128)(2,1)S(1)}, u32[]{:S(2)}, u32[]{:S(2)}) collective-permute-start(bf16[4,1,8,16]{3,2,1,0:T(8,128)(2,1)S(1)} %get-tuple-element.151), channel_id=1, source_target_pairs={{1,0},{2,1},{3,2},{5,4},{6,5},{7,6},{9,8},{10,9},{11,10},{13,12},{... | collective-permute-start | bytes 3080 | tf_op jit(solution)/shard_map/ppermute | solution.py:33
  29.8 5.9 %collective-permute-start.1 = (bf16[4,1,8,16]{3,2,1,0:T(8,128)(2,1)S(1)}, bf16[4,1,8,16]{3,2,1,0:T(8,128)(2,1)S(1)}, u32[]{:S(2)}, u32[]{:S(2)}) collective-permute-start(bf16[4,1,8,16]{3,2,1,0:T(8,128)(2,1)S(1)} %get-tuple-element.150), channel_id=1, source_target_pairs={{0,1},{1,2},{2,3},{4,5},{5,6},{6,7},{8,9},{9,10},{10,11},{12,13},{... | collective-permute-start | bytes 3080 | tf_op jit(solution)/shard_map/ppermute | solution.py:30
  41.0 8.0 %collective-permute-start.3 = (bf16[2,8,8,384]{3,2,1,0:T(8,128)(2,1)S(1)}, bf16[2,8,8,384]{3,2,1,0:T(8,128)(2,1)S(1)}, u32[]{:S(2)}, u32[]{:S(2)}) collective-permute-start(bf16[2,8,8,384]{3,2,1,0:T(8,128)(2,1)S(1)} %multiply_convert_fusion), channel_id=1, source_target_pairs={{0,4},{4,8},{8,12},{12,16},{16,20},{20,24},{24,28},{28,32},{32,36}... | collective-permute-start | bytes 294920 | tf_op jit(solution)/shard_map/ppermute | solution.py:22
  49.1 8.2 %collective-permute-start.5 = (bf16[4,1,8,384]{3,2,1,0:T(8,128)(2,1)S(1)}, bf16[4,1,8,384]{3,2,1,0:T(8,128)(2,1)S(1)}, u32[]{:S(2)}, u32[]{:S(2)}) collective-permute-start(bf16[4,1,8,384]{3,2,1,0:T(8,128)(2,1)S(1)} %get-tuple-element.123), channel_id=1, source_target_pairs={{1,0},{2,1},{3,2},{5,4},{6,5},{7,6},{9,8},{10,9},{11,10},{13,12},{... | collective-permute-start | bytes 73736 | tf_op jit(solution)/shard_map/ppermute | solution.py:33
  50.4 6.9 %collective-permute-start.4 = (bf16[4,1,8,384]{3,2,1,0:T(8,128)(2,1)S(1)}, bf16[4,1,8,384]{3,2,1,0:T(8,128)(2,1)S(1)}, u32[]{:S(2)}, u32[]{:S(2)}) collective-permute-start(bf16[4,1,8,384]{3,2,1,0:T(8,128)(2,1)S(1)} %get-tuple-element.122), channel_id=1, source_target_pairs={{0,1},{1,2},{2,3},{4,5},{5,6},{6,7},{8,9},{9,10},{10,11},{12,13},{... | collective-permute-start | bytes 73736 | tf_op jit(solution)/shard_map/ppermute | solution.py:30
  57.3 15.1 %copy-start.18 = (f32[384]{0:T(512)S(1)}, f32[384]{0:T(512)}, u32[]{:S(2)}) copy-start(f32[384]{0:T(512)} %param.21) | copy-start | bytes 4612
  107.5 28.3 %collective-permute-start.19 = (bf16[24576]{0:T(1024)(128)(2,1)S(1)}, bf16[24576]{0:T(1024)(128)(2,1)S(1)}, u32[]{:S(2)}, u32[]{:S(2)}) collective-permute-start(bf16[24576]{0:T(1024)(128)(2,1)S(1)} %convert_element_type.401), channel_id=1, source_target_pairs={{0,28},{4,32},{8,36},{12,40},{16,44},{20,48},{24,52},{28,56},{32,6... | collective-permute-start | bytes 147464 | tf_op jit(solution)/shard_map/ppermute | solution.py:22
  112.4 26.0 %collective-permute-start.18 = (bf16[24576]{0:T(1024)(128)(2,1)S(1)}, bf16[24576]{0:T(1024)(128)(2,1)S(1)}, u32[]{:S(2)}, u32[]{:S(2)}) collective-permute-start(bf16[24576]{0:T(1024)(128)(2,1)S(1)} %convert_element_type.399), channel_id=1, source_target_pairs={{0,24},{4,28},{8,32},{12,36},{16,40},{20,44},{24,48},{28,52},{32,5... | collective-permute-start | bytes 147464 | tf_op jit(solution)/shard_map/ppermute | solution.py:22
  117.3 23.5 %collective-permute-start.17 = (bf16[24576]{0:T(1024)(128)(2,1)S(1)}, bf16[24576]{0:T(1024)(128)(2,1)S(1)}, u32[]{:S(2)}, u32[]{:S(2)}) collective-permute-start(bf16[24576]{0:T(1024)(128)(2,1)S(1)} %convert_element_type.397), channel_id=1, source_target_pairs={{0,20},{4,24},{8,28},{12,32},{16,36},{20,40},{24,44},{28,48},{32,5... | collective-permute-start | bytes 147464 | tf_op jit(solution)/shard_map/ppermute | solution.py:22
  121.1 25.0 %collective-permute-start.16 = (bf16[24576]{0:T(1024)(128)(2,1)S(1)}, bf16[24576]{0:T(1024)(128)(2,1)S(1)}, u32[]{:S(2)}, u32[]{:S(2)}) collective-permute-start(bf16[24576]{0:T(1024)(128)(2,1)S(1)} %convert_element_type.395), channel_id=1, source_target_pairs={{0,16},{4,20},{8,24},{12,28},{16,32},{20,36},{24,40},{28,44},{32,4... | collective-permute-start | bytes 147464 | tf_op jit(solution)/shard_map/ppermute | solution.py:22
  125.6 24.8 %collective-permute-start.15 = (bf16[24576]{0:T(1024)(128)(2,1)S(1)}, bf16[24576]{0:T(1024)(128)(2,1)S(1)}, u32[]{:S(2)}, u32[]{:S(2)}) collective-permute-start(bf16[24576]{0:T(1024)(128)(2,1)S(1)} %convert_element_type.393), channel_id=1, source_target_pairs={{0,12},{4,16},{8,20},{12,24},{16,28},{20,32},{24,36},{28,40},{32,4... | collective-permute-start | bytes 147464 | tf_op jit(solution)/shard_map/ppermute | solution.py:22
  135.8 16.6 %collective-permute-start.14 = (bf16[24576]{0:T(1024)(128)(2,1)S(1)}, bf16[24576]{0:T(1024)(128)(2,1)S(1)}, u32[]{:S(2)}, u32[]{:S(2)}) collective-permute-start(bf16[24576]{0:T(1024)(128)(2,1)S(1)} %convert_element_type.391), channel_id=1, source_target_pairs={{0,8},{4,12},{8,16},{12,20},{16,24},{20,28},{24,32},{28,36},{32,40... | collective-permute-start | bytes 147464 | tf_op jit(solution)/shard_map/ppermute | solution.py:22
  138.4 16.1 %collective-permute-start.13 = (bf16[24576]{0:T(1024)(128)(2,1)S(1)}, bf16[24576]{0:T(1024)(128)(2,1)S(1)}, u32[]{:S(2)}, u32[]{:S(2)}) collective-permute-start(bf16[24576]{0:T(1024)(128)(2,1)S(1)} %convert_element_type.389), channel_id=1, source_target_pairs={{0,4},{4,8},{8,12},{12,16},{16,20},{20,24},{24,28},{28,32},{32,36}... | collective-permute-start | bytes 147464 | tf_op jit(solution)/shard_map/ppermute | solution.py:22
  140.8 17.6 %collective-permute-start.12 = (bf16[24576]{0:T(1024)(128)(2,1)S(1)}, bf16[24576]{0:T(1024)(128)(2,1)S(1)}, u32[]{:S(2)}, u32[]{:S(2)}) collective-permute-start(bf16[24576]{0:T(1024)(128)(2,1)S(1)} %convert_element_type.387), channel_id=1, source_target_pairs={{4,0},{8,4},{12,8},{16,12},{20,16},{24,20},{28,24},{32,28},{36,32}... | collective-permute-start | bytes 147464 | tf_op jit(solution)/shard_map/ppermute | solution.py:22
  146.1 14.2 %collective-permute-start.11 = (bf16[24576]{0:T(1024)(128)(2,1)S(1)}, bf16[24576]{0:T(1024)(128)(2,1)S(1)}, u32[]{:S(2)}, u32[]{:S(2)}) collective-permute-start(bf16[24576]{0:T(1024)(128)(2,1)S(1)} %convert_element_type.385), channel_id=1, source_target_pairs={{8,0},{12,4},{16,8},{20,12},{24,16},{28,20},{32,24},{36,28},{40,32... | collective-permute-start | bytes 147464 | tf_op jit(solution)/shard_map/ppermute | solution.py:22
  150.4 32.2 %copy-start.6 = (f32[1,1024]{1,0:T(1,128)S(1)}, f32[1,1024]{1,0:T(1,128)}, u32[]{:S(2)}) copy-start(f32[1,1024]{1,0:T(1,128)} %get-tuple-element.155) | copy-start | bytes 12292
  150.4 12.8 %collective-permute-start.10 = (bf16[24576]{0:T(1024)(128)(2,1)S(1)}, bf16[24576]{0:T(1024)(128)(2,1)S(1)}, u32[]{:S(2)}, u32[]{:S(2)}) collective-permute-start(bf16[24576]{0:T(1024)(128)(2,1)S(1)} %convert_element_type.383), channel_id=1, source_target_pairs={{12,0},{16,4},{20,8},{24,12},{28,16},{32,20},{36,24},{40,28},{44,3... | collective-permute-start | bytes 147464 | tf_op jit(solution)/shard_map/ppermute | solution.py:22
  152.4 10.8 %collective-permute-start.9 = (bf16[24576]{0:T(1024)(128)(2,1)S(1)}, bf16[24576]{0:T(1024)(128)(2,1)S(1)}, u32[]{:S(2)}, u32[]{:S(2)}) collective-permute-start(bf16[24576]{0:T(1024)(128)(2,1)S(1)} %convert_element_type.381), channel_id=1, source_target_pairs={{16,0},{20,4},{24,8},{28,12},{32,16},{36,20},{40,24},{44,28},{48,3... | collective-permute-start | bytes 147464 | tf_op jit(solution)/shard_map/ppermute | solution.py:22
  154.5 8.7 %collective-permute-start.8 = (bf16[24576]{0:T(1024)(128)(2,1)S(1)}, bf16[24576]{0:T(1024)(128)(2,1)S(1)}, u32[]{:S(2)}, u32[]{:S(2)}) collective-permute-start(bf16[24576]{0:T(1024)(128)(2,1)S(1)} %convert_element_type.379), channel_id=1, source_target_pairs={{20,0},{24,4},{28,8},{32,12},{36,16},{40,20},{44,24},{48,28},{52,3... | collective-permute-start | bytes 147464 | tf_op jit(solution)/shard_map/ppermute | solution.py:22
  158.4 8.4 %collective-permute-start.7 = (bf16[24576]{0:T(1024)(128)(2,1)S(1)}, bf16[24576]{0:T(1024)(128)(2,1)S(1)}, u32[]{:S(2)}, u32[]{:S(2)}) collective-permute-start(bf16[24576]{0:T(1024)(128)(2,1)S(1)} %convert_element_type.377), channel_id=1, source_target_pairs={{24,0},{28,4},{32,8},{36,12},{40,16},{44,20},{48,24},{52,28},{56,3... | collective-permute-start | bytes 147464 | tf_op jit(solution)/shard_map/ppermute | solution.py:22
  160.4 9.0 %collective-permute-start.6 = (bf16[24576]{0:T(1024)(128)(2,1)S(1)}, bf16[24576]{0:T(1024)(128)(2,1)S(1)}, u32[]{:S(2)}, u32[]{:S(2)}) collective-permute-start(bf16[24576]{0:T(1024)(128)(2,1)S(1)} %convert_element_type.375), channel_id=1, source_target_pairs={{28,0},{32,4},{36,8},{40,12},{44,16},{48,20},{52,24},{56,28},{60,3... | collective-permute-start | bytes 147464 | tf_op jit(solution)/shard_map/ppermute | solution.py:22
  169.6 13.0 %copy-start.1 = (bf16[1024,768]{1,0:T(8,128)(2,1)S(1)}, bf16[1024,768]{1,0:T(8,128)(2,1)}, u32[]{:S(2)}) copy-start(bf16[1024,768]{1,0:T(8,128)(2,1)} %param.27) | copy-start | bytes 4718596
  186.9 48.2 %copy-start.5 = (bf16[64,4,1,64]{0,3,1,2:T(8,128)(2,1)S(1)}, bf16[64,4,1,64]{0,3,1,2:T(8,128)(2,1)}, u32[]{:S(2)}) copy-start(bf16[64,4,1,64]{0,3,1,2:T(8,128)(2,1)} %copy.271) | copy-start | bytes 98308
  191.9 77.1 %reduce-scatter.5.cloned.1.call-start = ((), (), s32[]{:S(2)}) async-start(), calls=%async_computation.6 | async-start | bytes 163840 | tf_op jit(solution)/shard_map/reduce_scatter | solution.py:218
  195.0 36.9 %copy-start.16 = (f32[1024]{0:T(1024)}, f32[1024]{0:T(1024)S(1)}, u32[]{:S(2)}) copy-start(f32[1024]{0:T(1024)S(1)} %broadcast_subtract_fusion) | copy-start | bytes 12292
  216.3 15.6 %copy-start.20 = (f32[16]{0:T(128)}, f32[16]{0:T(128)S(1)}, u32[]{:S(2)}) copy-start(f32[16]{0:T(128)S(1)} %broadcast_multiply_fusion.6) | copy-start | bytes 196
  217.3 14.7 %copy-start.21 = (f32[16]{0:T(128)}, f32[16]{0:T(128)S(1)}, u32[]{:S(2)}) copy-start(f32[16]{0:T(128)S(1)} %add_rsqrt_fusion.1) | copy-start | bytes 196
  233.4 36.5 %copy-start.3 = (bf16[16,1024]{1,0:T(8,128)(2,1)S(1)}, bf16[16,1024]{1,0:T(8,128)(2,1)}, u32[]{:S(2)}) copy-start(bf16[16,1024]{1,0:T(8,128)(2,1)} %reduce-scatter.3.cloned.1.call-done) | copy-start | bytes 98308
  240.4 28.6 %copy-start.23 = (f32[16]{0:T(128)S(1)}, f32[16]{0:T(128)}, u32[]{:S(2)}) copy-start(f32[16]{0:T(128)} %copy-done.22) | copy-start | bytes 196
  272.4 17.5 %collective-permute-start.33 = (bf16[24576]{0:T(1024)(128)(2,1)}, bf16[24576]{0:T(1024)(128)(2,1)S(1)}, u32[]{:S(2)}, u32[]{:S(2)}) collective-permute-start(bf16[24576]{0:T(1024)(128)(2,1)} %reshape_reshape.8), channel_id=1, source_target_pairs={{28,0},{32,4},{36,8},{40,12},{44,16},{48,20},{52,24},{56,28},{60,3... | collective-permute-start | bytes 147464 | tf_op jit(solution)/shard_map/ppermute | solution.py:22
  277.2 14.9 %collective-permute-start.32 = (bf16[24576]{0:T(1024)(128)(2,1)}, bf16[24576]{0:T(1024)(128)(2,1)S(1)}, u32[]{:S(2)}, u32[]{:S(2)}) collective-permute-start(bf16[24576]{0:T(1024)(128)(2,1)} %reshape_reshape.8), channel_id=1, source_target_pairs={{24,0},{28,4},{32,8},{36,12},{40,16},{44,20},{48,24},{52,28},{56,3... | collective-permute-start | bytes 147464 | tf_op jit(solution)/shard_map/ppermute | solution.py:22
  281.1 13.0 %collective-permute-start.31 = (bf16[24576]{0:T(1024)(128)(2,1)}, bf16[24576]{0:T(1024)(128)(2,1)S(1)}, u32[]{:S(2)}, u32[]{:S(2)}) collective-permute-start(bf16[24576]{0:T(1024)(128)(2,1)} %reshape_reshape.8), channel_id=1, source_target_pairs={{20,0},{24,4},{28,8},{32,12},{36,16},{40,20},{44,24},{48,28},{52,3... | collective-permute-start | bytes 147464 | tf_op jit(solution)/shard_map/ppermute | solution.py:22
  283.9 12.5 %collective-permute-start.30 = (bf16[24576]{0:T(1024)(128)(2,1)}, bf16[24576]{0:T(1024)(128)(2,1)S(1)}, u32[]{:S(2)}, u32[]{:S(2)}) collective-permute-start(bf16[24576]{0:T(1024)(128)(2,1)} %reshape_reshape.8), channel_id=1, source_target_pairs={{16,0},{20,4},{24,8},{28,12},{32,16},{36,20},{40,24},{44,28},{48,3... | collective-permute-start | bytes 147464 | tf_op jit(solution)/shard_map/ppermute | solution.py:22
  287.9 14.0 %collective-permute-start.29 = (bf16[24576]{0:T(1024)(128)(2,1)}, bf16[24576]{0:T(1024)(128)(2,1)S(1)}, u32[]{:S(2)}, u32[]{:S(2)}) collective-permute-start(bf16[24576]{0:T(1024)(128)(2,1)} %reshape_reshape.8), channel_id=1, source_target_pairs={{12,0},{16,4},{20,8},{24,12},{28,16},{32,20},{36,24},{40,28},{44,3... | collective-permute-start | bytes 147464 | tf_op jit(solution)/shard_map/ppermute | solution.py:22
  289.9 38.6 %copy-start.7 = (bf16[24576]{0:T(1024)(128)(2,1)}, bf16[24576]{0:T(1024)(128)(2,1)S(1)}, u32[]{:S(2)}) copy-start(bf16[24576]{0:T(1024)(128)(2,1)S(1)} %collective-permute-done.33) | copy-start | bytes 147460
  289.9 16.4 %collective-permute-start.28 = (bf16[24576]{0:T(1024)(128)(2,1)}, bf16[24576]{0:T(1024)(128)(2,1)S(1)}, u32[]{:S(2)}, u32[]{:S(2)}) collective-permute-start(bf16[24576]{0:T(1024)(128)(2,1)} %reshape_reshape.8), channel_id=1, source_target_pairs={{8,0},{12,4},{16,8},{20,12},{24,16},{28,20},{32,24},{36,28},{40,32... | collective-permute-start | bytes 147464 | tf_op jit(solution)/shard_map/ppermute | solution.py:22
  292.1 36.4 %copy-start.8 = (bf16[24576]{0:T(1024)(128)(2,1)}, bf16[24576]{0:T(1024)(128)(2,1)S(1)}, u32[]{:S(2)}) copy-start(bf16[24576]{0:T(1024)(128)(2,1)S(1)} %collective-permute-done.32) | copy-start | bytes 147460
  292.1 19.9 %collective-permute-start.27 = (bf16[24576]{0:T(1024)(128)(2,1)}, bf16[24576]{0:T(1024)(128)(2,1)S(1)}, u32[]{:S(2)}, u32[]{:S(2)}) collective-permute-start(bf16[24576]{0:T(1024)(128)(2,1)} %reshape_reshape.8), channel_id=1, source_target_pairs={{4,0},{8,4},{12,8},{16,12},{20,16},{24,20},{28,24},{32,28},{36,32}... | collective-permute-start | bytes 147464 | tf_op jit(solution)/shard_map/ppermute | solution.py:22
  294.1 34.4 %copy-start.9 = (bf16[24576]{0:T(1024)(128)(2,1)}, bf16[24576]{0:T(1024)(128)(2,1)S(1)}, u32[]{:S(2)}) copy-start(bf16[24576]{0:T(1024)(128)(2,1)S(1)} %collective-permute-done.31) | copy-start | bytes 147460
  294.1 21.9 %collective-permute-start.26 = (bf16[24576]{0:T(1024)(128)(2,1)}, bf16[24576]{0:T(1024)(128)(2,1)S(1)}, u32[]{:S(2)}, u32[]{:S(2)}) collective-permute-start(bf16[24576]{0:T(1024)(128)(2,1)} %reshape_reshape.8), channel_id=1, source_target_pairs={{0,4},{4,8},{8,12},{12,16},{16,20},{20,24},{24,28},{28,32},{32,36}... | collective-permute-start | bytes 147464 | tf_op jit(solution)/shard_map/ppermute | solution.py:22
  296.5 32.0 %copy-start.10 = (bf16[24576]{0:T(1024)(128)(2,1)}, bf16[24576]{0:T(1024)(128)(2,1)S(1)}, u32[]{:S(2)}) copy-start(bf16[24576]{0:T(1024)(128)(2,1)S(1)} %collective-permute-done.30) | copy-start | bytes 147460
  296.5 27.0 %collective-permute-start.25 = (bf16[24576]{0:T(1024)(128)(2,1)}, bf16[24576]{0:T(1024)(128)(2,1)S(1)}, u32[]{:S(2)}, u32[]{:S(2)}) collective-permute-start(bf16[24576]{0:T(1024)(128)(2,1)} %reshape_reshape.8), channel_id=1, source_target_pairs={{0,8},{4,12},{8,16},{12,20},{16,24},{20,28},{24,32},{28,36},{32,40... | collective-permute-start | bytes 147464 | tf_op jit(solution)/shard_map/ppermute | solution.py:22
  302.0 26.5 %copy-start.11 = (bf16[24576]{0:T(1024)(128)(2,1)}, bf16[24576]{0:T(1024)(128)(2,1)S(1)}, u32[]{:S(2)}) copy-start(bf16[24576]{0:T(1024)(128)(2,1)S(1)} %collective-permute-done.29) | copy-start | bytes 147460
  302.0 39.8 %collective-permute-start.24 = (bf16[24576]{0:T(1024)(128)(2,1)}, bf16[24576]{0:T(1024)(128)(2,1)}, u32[]{:S(2)}, u32[]{:S(2)}) collective-permute-start(bf16[24576]{0:T(1024)(128)(2,1)} %reshape_reshape.8), channel_id=1, source_target_pairs={{0,12},{4,16},{8,20},{12,24},{16,28},{20,32},{24,36},{28,40},{32,4... | collective-permute-start | bytes 147464 | tf_op jit(solution)/shard_map/ppermute | solution.py:22
  306.3 22.2 %copy-start.12 = (bf16[24576]{0:T(1024)(128)(2,1)}, bf16[24576]{0:T(1024)(128)(2,1)S(1)}, u32[]{:S(2)}) copy-start(bf16[24576]{0:T(1024)(128)(2,1)S(1)} %collective-permute-done.28) | copy-start | bytes 147460
  306.3 37.0 %collective-permute-start.23 = (bf16[24576]{0:T(1024)(128)(2,1)}, bf16[24576]{0:T(1024)(128)(2,1)}, u32[]{:S(2)}, u32[]{:S(2)}) collective-permute-start(bf16[24576]{0:T(1024)(128)(2,1)} %reshape_reshape.8), channel_id=1, source_target_pairs={{0,16},{4,20},{8,24},{12,28},{16,32},{20,36},{24,40},{28,44},{32,4... | collective-permute-start | bytes 147464 | tf_op jit(solution)/shard_map/ppermute | solution.py:22
  312.0 16.5 %copy-start.13 = (bf16[24576]{0:T(1024)(128)(2,1)}, bf16[24576]{0:T(1024)(128)(2,1)S(1)}, u32[]{:S(2)}) copy-start(bf16[24576]{0:T(1024)(128)(2,1)S(1)} %collective-permute-done.27) | copy-start | bytes 147460
  312.0 32.8 %collective-permute-start.22 = (bf16[24576]{0:T(1024)(128)(2,1)}, bf16[24576]{0:T(1024)(128)(2,1)}, u32[]{:S(2)}, u32[]{:S(2)}) collective-permute-start(bf16[24576]{0:T(1024)(128)(2,1)} %reshape_reshape.8), channel_id=1, source_target_pairs={{0,20},{4,24},{8,28},{12,32},{16,36},{20,40},{24,44},{28,48},{32,5... | collective-permute-start | bytes 147464 | tf_op jit(solution)/shard_map/ppermute | solution.py:22
  316.1 30.2 %collective-permute-start.21 = (bf16[24576]{0:T(1024)(128)(2,1)}, bf16[24576]{0:T(1024)(128)(2,1)}, u32[]{:S(2)}, u32[]{:S(2)}) collective-permute-start(bf16[24576]{0:T(1024)(128)(2,1)} %reshape_reshape.8), channel_id=1, source_target_pairs={{0,24},{4,28},{8,32},{12,36},{16,40},{20,44},{24,48},{28,52},{32,5... | collective-permute-start | bytes 147464 | tf_op jit(solution)/shard_map/ppermute | solution.py:22
  323.5 24.2 %collective-permute-start.20 = (bf16[24576]{0:T(1024)(128)(2,1)}, bf16[24576]{0:T(1024)(128)(2,1)}, u32[]{:S(2)}, u32[]{:S(2)}) collective-permute-start(bf16[24576]{0:T(1024)(128)(2,1)} %reshape_reshape.8), channel_id=1, source_target_pairs={{0,28},{4,32},{8,36},{12,40},{16,44},{20,48},{24,52},{28,56},{32,6... | collective-permute-start | bytes 147464 | tf_op jit(solution)/shard_map/ppermute | solution.py:22
  359.2 7.1 %collective-permute-start.34 = (f32[4,8,384]{2,1,0:T(8,128)}, f32[4,8,384]{2,1,0:T(8,128)S(1)}, u32[]{:S(2)}, u32[]{:S(2)}) collective-permute-start(f32[4,8,384]{2,1,0:T(8,128)} %get-tuple-element.87), channel_id=1, source_target_pairs={{1,0},{2,1},{3,2},{5,4},{6,5},{7,6},{9,8},{10,9},{11,10},{13,12},{... | collective-permute-start | bytes 147464 | tf_op jit(solution)/shard_map/ppermute | solution.py:22
  360.5 15.0 %copy-start.4 = (bf16[432,384]{1,0:T(8,128)(2,1)S(1)}, bf16[432,384]{1,0:T(8,128)(2,1)}, u32[]{:S(2)}) copy-start(bf16[432,384]{1,0:T(8,128)(2,1)} %param.20) | copy-start | bytes 995332
  360.5 15.0 %copy-start.19 = (f32[384]{0:T(512)S(1)}, f32[384]{0:T(512)}, u32[]{:S(2)}) copy-start(f32[384]{0:T(512)} %param.21) | copy-start | bytes 4612
  361.8 6.3 %collective-permute-start.35 = (f32[4,8,384]{2,1,0:T(8,128)S(1)}, f32[4,8,384]{2,1,0:T(8,128)S(1)}, u32[]{:S(2)}, u32[]{:S(2)}) collective-permute-start(f32[4,8,384]{2,1,0:T(8,128)S(1)} %get-tuple-element.86), channel_id=1, source_target_pairs={{0,1},{1,2},{2,3},{4,5},{5,6},{6,7},{8,9},{9,10},{10,11},{12,13},{... | collective-permute-start | bytes 147464 | tf_op jit(solution)/shard_map/ppermute | solution.py:22
  368.1 6.5 %collective-permute-start.36 = (bf16[2,8,8,384]{3,2,1,0:T(8,128)(2,1)S(1)}, bf16[2,8,8,384]{3,2,1,0:T(8,128)(2,1)S(1)}, u32[]{:S(2)}, u32[]{:S(2)}) collective-permute-start(bf16[2,8,8,384]{3,2,1,0:T(8,128)(2,1)S(1)} %fusion.47), channel_id=1, source_target_pairs={{4,0},{8,4},{12,8},{16,12},{20,16},{24,20},{28,24},{32,28},{36,32}... | collective-permute-start | bytes 294920 | tf_op jit(solution)/shard_map/ppermute | solution.py:22
  376.8 5.9 %collective-permute-start.37 = (f32[4,8,16]{2,1,0:T(8,128)S(1)}, f32[4,8,16]{2,1,0:T(8,128)S(1)}, u32[]{:S(2)}, u32[]{:S(2)}) collective-permute-start(f32[4,8,16]{2,1,0:T(8,128)S(1)} %get-tuple-element.89), channel_id=1, source_target_pairs={{1,0},{2,1},{3,2},{5,4},{6,5},{7,6},{9,8},{10,9},{11,10},{13,12},{... | collective-permute-start | bytes 6152 | tf_op jit(solution)/shard_map/ppermute | solution.py:22
  378.1 6.0 %collective-permute-start.38 = (f32[4,8,16]{2,1,0:T(8,128)S(1)}, f32[4,8,16]{2,1,0:T(8,128)S(1)}, u32[]{:S(2)}, u32[]{:S(2)}) collective-permute-start(f32[4,8,16]{2,1,0:T(8,128)S(1)} %get-tuple-element.88), channel_id=1, source_target_pairs={{0,1},{1,2},{2,3},{4,5},{5,6},{6,7},{8,9},{9,10},{10,11},{12,13},{... | collective-permute-start | bytes 6152 | tf_op jit(solution)/shard_map/ppermute | solution.py:22
  384.1 6.6 %collective-permute-start.39 = (bf16[2,8,8,16]{3,2,0,1:T(8,128)(2,1)S(1)}, bf16[2,8,8,16]{3,2,0,1:T(8,128)(2,1)S(1)}, u32[]{:S(2)}, u32[]{:S(2)}) collective-permute-start(bf16[2,8,8,16]{3,2,0,1:T(8,128)(2,1)S(1)} %fusion.70), channel_id=1, source_target_pairs={{4,0},{8,4},{12,8},{16,12},{20,16},{24,20},{28,24},{32,28},{36,32}... | collective-permute-start | bytes 12296 | tf_op jit(solution)/shard_map/ppermute | solution.py:22
  391.7 17.8 %all-to-all-start.1 = ((f32[4,1,512]{2,1,0:T(1,128)}), f32[4,1,512]{2,1,0:T(1,128)S(1)}, u32[]{:S(2)}, u32[]{:S(2)}) async-start(f32[4,1,512]{2,1,0:T(1,128)} %reshape.750), calls=%async_computation.3 | async-start | bytes 16384 | tf_op jit(solution)/shard_map/all_to_all | solution.py:290
  (8 other events, 50.6 us)
Sparse Core Ops, SparseCore 0:
  9.8 85.7 all-gather.1
  192.0 23.4 reduce-scatter.2
  246.2 22.6 reduce-scatter.4
where the time goes:
time: 422 us; the launch traced here: 418 us
  starting transfers between devices  145 us (34%)
  waiting for transfers between devices  84.3 us (20%)
  local copies, waits for them, and re-layouts  59.3 us (14%)
  matrix products  42.9 us (10%)
  blocking collectives  36.4 us (9%)
  other arithmetic  33.3 us (8%)
  between operations  17 us (4%)
    ppermute x36, starting transfers between devices, passed_along(): lax.ppermute(value, axis, [(source, source + steps) for source in range(l...  123 us
    ppermute x36, waiting for transfers between devices, passed_along(): lax.ppermute(value, axis, [(source, source + steps) for source in range(l...  21.1 us
    reduce_scatter x1, waiting for transfers between devices, score_frame(): lax.psum_scatter(contract_last(grad_qkv, qkv_weight).astype(jnp.bfloat16)...  21.1 us
    mul x14, local copies, waits for them, and re-layouts, incoming(): return hit_rows[:, None] * source_grad[None, :].astype(jnp.float32)  20.5 us
    reduce_scatter x1, waiting for transfers between devices, score_frame(): lax.psum_scatter(jnp.dot(mixed, out_weight, preferred_element_type=jnp.fl...  20.4 us
    unnamed x85, local copies, waits for them, and re-layouts  20.2 us
    all_gather x1, waiting for transfers between devices, body(): whole_conv = lax.all_gather(conv_weight, 'sp', axis=1, tiled=True)  19.6 us
    convert_element_type x8, other arithmetic, incoming(): hit_rows = (own_frames == frame_index).astype(jnp.float32)  13.9 us
  transfers between devices with their start and end apart: 45, of which 12 were waited for; matrix products, arithmetic and copies ran while one was open for 18% of the time, Pallas kernels for 0%

commit v1 on v0

v1 whole, which is shorter than its diff:
```python
import functools

import jax
import jax.numpy as jnp
from jax import lax
from jax.experimental import pallas as pl
from jax.experimental.pallas import tpu as pltpu
from jax.sharding import PartitionSpec as P

LAT = 16
CH = 384
VW = 1024
HD = 64
COLS = 8
ROWS = 32
CLIP_FR = 16
FR_DEV = 2
CLIP_DEV = CLIP_FR // FR_DEV
SP = 4
OUT_CH = CH // SP
LOCAL_HEADS = 4
TOKENS = 64
CELLS = ROWS * COLS
HALF = 64
MESH = pl.DeviceIdType.MESH

norm_epsilon = 1e-06
layer_epsilon = 1e-05

f32 = jnp.float32
bf16 = jnp.bfloat16


def dot(left, right):
    return lax.dot_general(left, right, (((1,), (0,)), ((), ())), preferred_element_type=f32)


def dot_last(left, right):
    return lax.dot_general(left, right, (((1,), (1,)), ((), ())), preferred_element_type=f32)


def dot_first(left, right):
    return lax.dot_general(left, right, (((0,), (0,)), ((), ())), preferred_element_type=f32)


def iota(shape, dim):
    return lax.broadcasted_iota(jnp.int32, shape, dim)


def one_hot(condition):
    return jnp.where(condition, 1.0, 0.0).astype(bf16)


def row_mean(value):
    return jnp.sum(value, axis=-1, keepdims=True) * (1.0 / value.shape[-1])


def layer_stats(volume):
    center = row_mean(volume)
    moved = volume - center
    inverse = lax.rsqrt(row_mean(moved * moved) + layer_epsilon)
    return moved * inverse, inverse


def layer_back(whitened, inverse, scaled_grad):
    return inverse * (
        scaled_grad - row_mean(scaled_grad) - whitened * row_mean(scaled_grad * whitened)
    )


def shifted(value, offset):
    if offset == 0:
        return value
    blank = jnp.zeros(value.shape[:-2] + (1, value.shape[-1]), value.dtype)
    if offset > 0:
        return jnp.concatenate([value[..., 1:, :], blank], axis=-2)
    return jnp.concatenate([blank, value[..., :-1, :]], axis=-2)


def spread(pick, dst, send, recv, count, here, place):
    copies = []
    for step in range(1, count):
        peer = lax.rem(here + step, count)
        copy = pltpu.make_async_remote_copy(
            src_ref=pick(peer),
            dst_ref=dst.at[here],
            send_sem=send.at[step],
            recv_sem=recv.at[step],
            device_id=place(peer),
            device_id_type=MESH,
        )
        copy.start()
        copies.append(copy)
    return copies


def wait_all(copies):
    for copy in copies:
        copy.wait()


def kernel(
    lat_ref,
    list_ref,
    scale_ref,
    gain_ref,
    wi_ref,
    ln_ref,
    head_ref,
    wc_hbm,
    pw_hbm,
    qw_hbm,
    ow_hbm,
    grad_ref,
    reward_ref,
    wc,
    pw,
    qw,
    ow,
    wi_pad,
    lat_seq,
    lat_sp,
    z_ref,
    rolled,
    cols,
    first,
    act,
    feat,
    part,
    rim,
    patch_out,
    patch_in,
    lat_back,
    band_out,
    band_in,
    placed,
    clip_out,
    clip_in,
    back_cols,
    load_sem,
    seq_sems,
    sp_sems,
):
    seq = lax.axis_index("seq")
    sp = lax.axis_index("sp")
    local = lax.rem(seq, CLIP_DEV)
    base = seq - local

    def in_clip(peer):
        return (base + peer, sp)

    def in_band(peer):
        return (seq, peer)

    barrier = pltpu.get_barrier_semaphore()
    for step in range(1, CLIP_DEV):
        pl.semaphore_signal(
            barrier,
            inc=1,
            device_id=in_clip(lax.rem(local + step, CLIP_DEV)),
            device_id_type=MESH,
        )
    for step in range(1, SP):
        pl.semaphore_signal(
            barrier, inc=1, device_id=in_band(lax.rem(sp + step, SP)), device_id_type=MESH
        )
    loads = [
        pltpu.make_async_copy(source, target, load_sem.at[i])
        for i, (source, target) in enumerate(
            ((wc_hbm, wc), (pw_hbm, pw), (qw_hbm, qw), (ow_hbm, ow))
        )
    ]
    for load in loads:
        load.start()

    lat_seq[0:2] = jnp.zeros((2, 16, 128), bf16)
    own = lat_ref[...].reshape(FR_DEV * ROWS, 32)
    packed = jnp.zeros((16, 128), f32)
    for j in range(4):
        spot = one_hot(iota((32, 128), 1) == iota((32, 128), 0) + 32 * j)
        packed = packed + dot(own[16 * j : 16 * j + 16], spot)
    lat_seq[pl.ds(2 + local, 1)] = packed.astype(bf16)[None]

    pl.semaphore_wait(barrier, CLIP_DEV - 1 + SP - 1)

    copies = []
    for step in range(1, CLIP_DEV):
        peer = lax.rem(local + step, CLIP_DEV)
        copy = pltpu.make_async_remote_copy(
            src_ref=lat_seq.at[pl.ds(2 + local, 1)],
            dst_ref=lat_seq.at[pl.ds(2 + local, 1)],
            send_sem=seq_sems.at[0, step],
            recv_sem=seq_sems.at[1, step],
            device_id=in_clip(peer),
            device_id_type=MESH,
        )
        copy.start()
        copies.append(copy)

    wi_pad[...] = jnp.zeros((640, CH), bf16)
    for tap in range(9):
        start = 128 * (tap // 2) + HALF * (tap % 2)
        wi_pad[start : start + 48] = wi_ref[48 * tap : 48 * tap + 48]
    act[...] = jnp.zeros(act.shape, bf16)
    rim[...] = jnp.zeros(rim.shape, bf16)
    lat_back[...] = jnp.zeros(lat_back.shape, f32)
    placed[...] = jnp.zeros(placed.shape, f32)
    row, col = iota((512, 512), 0), iota((512, 512), 1)
    swap = one_hot(
        ((row >> 7) == ((col >> 5) & 3)) & (((row >> 5) & 3) == (col >> 7)) & ((row & 31) == (col & 31))
    )
    row, col = iota((256, 256), 0), iota((256, 256), 1)
    kind, token = row >> 6, row & 63
    to_patch = one_hot(
        col == (2 * (token >> 4) + (kind & 1)) * ROWS + 2 * (token & 15) + (kind >> 1)
    )
    own_channels = one_hot(iota((CH, OUT_CH), 0) == iota((CH, OUT_CH), 1) + sp * OUT_CH)

    wait_all(copies)

    where = lax.rem(list_ref[seq], CLIP_FR)
    chunk, odd = lax.div(where, 2), lax.rem(where, 2)
    lat_sp[pl.ds(sp, 1)] = lat_seq[pl.ds(chunk, 3)].reshape(1, 48, 128)
    copies = spread(
        lambda peer: lat_sp.at[sp], lat_sp, sp_sems.at[0], sp_sems.at[1], SP, sp, in_band
    )
    wait_all(copies)
    wide = jnp.concatenate([lat_sp[s] for s in range(SP)], axis=1)
    spots = dot(wide, swap)
    for c in range(3):
        for j in range(4):
            z_ref[2 * c + j // 2, 16 * (j % 2) : 16 * (j % 2) + 16] = spots[
                16 * c : 16 * c + 16, 128 * j : 128 * j + 128
            ]
    z = z_ref[pl.ds(odd, 5)]
    taps = jnp.stack([shifted(z, dr - 1) for dr in range(3)], axis=1).reshape(480, 128)
    for k in range(8):
        rolled[k] = (taps if k == 0 else pltpu.roll(taps, 16 * k, 1)).reshape(15, ROWS, 128)

    low_lanes = iota((ROWS, 128), 1) < HALF
    lane_col = (iota((ROWS, 128), 1) & (HALF - 1)) >> 4

    def build(c, carry):
        source_col = lane_col + (c - 1)
        inside = (source_col >= 0) & (source_col < COLS)
        even, second = lax.rem(9 - c, 8), lax.rem(13 - c, 8)
        for frame in range(3):
            for pair in range(5):
                tap = 2 * pair
                block = rolled[even, 3 * frame + tap]
                if tap + 1 < 9:
                    block = jnp.where(low_lanes, block, rolled[second, 3 * frame + tap + 1])
                cols[frame, c, :, 128 * pair : 128 * pair + 128] = jnp.where(
                    inside, block, 0.0
                ).astype(bf16)
        return carry

    lax.fori_loop(0, COLS, build, 0)

    gain = gain_ref[...]
    for frame in range(3):
        spots = dot(cols[frame].reshape(CELLS, 640), wi_pad[...])
        first[frame] = spots.astype(bf16).reshape(COLS, ROWS, CH)

    def activate(i, carry):
        frame, c = i // 2, lax.rem(i, 2) * 4
        h = first[frame, pl.ds(c, 4)].astype(f32)
        unit = h * lax.rsqrt(row_mean(h * h) + norm_epsilon) * gain
        value = unit * jax.nn.sigmoid(unit)
        for dr in range(3):
            act[dr, frame, pl.ds(c + 1, 4)] = shifted(value, dr - 1).astype(bf16)
        return carry

    lax.fori_loop(0, 6, activate, 0)

    loads[0].wait()
    total = dot(first[2].reshape(CELLS, CH), own_channels)
    for dt in range(3):
        for dr in range(3):
            window = jnp.concatenate(
                [act[dr, dt, dc : dc + COLS].reshape(CELLS, CH) for dc in range(3)], axis=1
            )
            start = (3 * dt + dr) * 3 * CH
            total = total + dot_last(window, wc[:, start : start + 3 * CH])
    feat[pl.ds(sp, 1)] = dot(to_patch, total.astype(bf16)).astype(bf16)[None]

    copies = spread(
        lambda peer: feat.at[sp], feat, sp_sems.at[2], sp_sems.at[3], SP, sp, in_band
    )
    loads[1].wait()
    loads[2].wait()
    loads[3].wait()
    wait_all(copies)

    patches = jnp.concatenate(
        [feat[s, TOKENS * k : TOKENS * k + TOKENS] for k in range(4) for s in range(SP)], axis=1
    )
    x = dot(patches, pw[...]).astype(bf16).astype(f32)
    white_in, inverse_in = layer_stats(x)
    gain_in, gain_out = ln_ref[0:1], ln_ref[1:2]
    qkv = dot((white_in * gain_in).astype(bf16), qw[...]).astype(bf16)
    heads = []
    mixed = []
    for head in range(LOCAL_HEADS):
        start = 3 * HD * head
        q, k, v = (qkv[:, start + HD * i : start + HD * i + HD] for i in range(3))
        scores = dot_last(q, k) * (HD**-0.5)
        weights = jnp.exp(scores - jnp.max(scores, axis=-1, keepdims=True))
        probs = weights / jnp.sum(weights, axis=-1, keepdims=True)
        probs_low = probs.astype(bf16)
        mixed.append(dot(probs_low, v).astype(bf16))
        heads.append((q, k, v, probs, probs_low))
    part[pl.ds(sp, 1)] = dot(jnp.concatenate(mixed, axis=1), ow[...]).astype(bf16)[None]
    copies = spread(
        lambda peer: part.at[sp], part, sp_sems.at[4], sp_sems.at[5], SP, sp, in_band
    )
    wait_all(copies)
    y = x
    for s in range(SP):
        y = y + part[s].astype(f32)
    white_out, inverse_out = layer_stats(y)
    vector = head_ref[...]
    reward = jnp.sum(white_out * gain_out * vector, axis=1, keepdims=True)
    reward_ref[...] = jnp.sum(reward, axis=0, keepdims=True) * (1.0 / TOKENS)
    scaled = (scale_ref[0] * (1.0 / TOKENS)) * vector * gain_out
    dy = layer_back(white_out, inverse_out, jnp.broadcast_to(scaled, y.shape))
    do = dot_last(dy.astype(bf16), ow[...]).astype(bf16)
    grads = []
    for head in range(LOCAL_HEADS):
        q, k, v, probs, probs_low = heads[head]
        d_out = do[:, HD * head : HD * head + HD]
        d_probs = dot_last(d_out, v)
        d_scores = (
            probs
            * (d_probs - jnp.sum(d_probs * probs, axis=-1, keepdims=True))
            * (HD**-0.5)
        ).astype(bf16)
        grads.append(dot(d_scores, k).astype(bf16))
        grads.append(dot_first(d_scores, q).astype(bf16))
        grads.append(dot_first(probs_low, d_out).astype(bf16))
    da = dot_last(jnp.concatenate(grads, axis=1), qw[...])
    dx = layer_back(white_in, inverse_in, da * gain_in) + dy * (1.0 / SP)
    d_patch = dot_last(dx.astype(bf16), pw[...]).astype(bf16)
    for s in range(SP):
        for k in range(4):
            start = CH * k + OUT_CH * s
            patch_out[s, TOKENS * k : TOKENS * k + TOKENS] = d_patch[:, start : start + OUT_CH]
    copies = spread(
        lambda peer: patch_out.at[peer], patch_in, sp_sems.at[6], sp_sems.at[7], SP, sp, in_band
    )
    patch_in[pl.ds(sp, 1)] = patch_out[pl.ds(sp, 1)]
    wait_all(copies)
    summed = patch_in[0].astype(f32)
    for s in range(1, SP):
        summed = summed + patch_in[s].astype(f32)
    d_feat = dot_first(to_patch, summed.astype(bf16))
    d_cells = d_feat.reshape(COLS, ROWS, OUT_CH)
    for dr in range(3):
        rim[dr, 1 : 1 + COLS] = shifted(d_cells, 1 - dr).astype(bf16)
    d_own = dot_last(d_feat.astype(bf16), own_channels)

    for frame in range(3):
        d_act = jnp.zeros((CELLS, CH), f32)
        for dr in range(3):
            for dc in range(3):
                start = ((3 * frame + dr) * 3 + dc) * CH
                d_act = d_act + dot(
                    rim[dr, 2 - dc : 2 - dc + COLS].reshape(CELLS, OUT_CH), wc[:, start : start + CH]
                )
        h = first[frame].reshape(CELLS, CH).astype(f32)
        inverse = lax.rsqrt(row_mean(h * h) + norm_epsilon)
        unit = h * inverse * gain
        gate = jax.nn.sigmoid(unit)
        d_unit = d_act * (gate * (1.0 + unit * (1.0 - gate))) * gain
        d_first = inverse * d_unit - h * (inverse * inverse * inverse * row_mean(d_unit * h))
        if frame == 2:
            d_first = d_first + d_own
        back_cols[frame] = dot_last(d_first.astype(bf16), wi_pad[...]).reshape(COLS, ROWS, 640)

    def collect(c, carry):
        source_col = lane_col + (c - 1)
        inside = (source_col >= 0) & (source_col < COLS)
        low = [jnp.zeros((ROWS, 128), f32)] * 15
        high = [jnp.zeros((ROWS, 128), f32)] * 15
        for frame in range(3):
            for pair in range(5):
                tap = 2 * pair
                block = jnp.where(inside, back_cols[frame, c, :, 128 * pair : 128 * pair + 128], 0.0)
                low[3 * frame + tap] = low[3 * frame + tap] + jnp.where(low_lanes, block, 0.0)
                if tap + 1 < 9:
                    high[3 * frame + tap + 1] = high[3 * frame + tap + 1] + jnp.where(
                        low_lanes, 0.0, block
                    )
        joined = jnp.concatenate(low, axis=0) + pltpu.roll(jnp.concatenate(high, axis=0), HALF, 1)
        return carry + pltpu.roll(joined, lax.rem(16 * c + 112, 128), 1)

    gathered = lax.fori_loop(0, COLS, collect, jnp.zeros((480, 128), f32))
    gathered = gathered.reshape(5, 3, ROWS, 128)
    lat_back[1:6] = (
        gathered[:, 1] + shifted(gathered[:, 0], 1) + shifted(gathered[:, 2], -1)
    )
    aligned = lat_back[pl.ds(1 - odd, 6)].astype(bf16)
    wide = jnp.concatenate(
        [
            jnp.concatenate(
                [aligned[2 * c + j // 2, 16 * (j % 2) : 16 * (j % 2) + 16] for j in range(4)], axis=1
            )
            for c in range(3)
        ],
        axis=0,
    )
    bands = dot(wide, swap).astype(bf16)
    for s in range(SP):
        band_out[s] = bands[:, 128 * s : 128 * s + 128]
    copies = spread(
        lambda peer: band_out.at[peer], band_in, sp_sems.at[8], sp_sems.at[9], SP, sp, in_band
    )
    band_in[pl.ds(sp, 1)] = band_out[pl.ds(sp, 1)]
    wait_all(copies)
    summed = band_in[0].astype(f32)
    for s in range(1, SP):
        summed = summed + band_in[s].astype(f32)
    placed[5:8] = summed.reshape(3, 16, 128)
    clip_out[...] = placed[pl.ds(7 - chunk, 8)].astype(bf16)
    copies = spread(
        lambda peer: clip_out.at[peer],
        clip_in,
        seq_sems.at[2],
        seq_sems.at[3],
        CLIP_DEV,
        local,
        in_clip,
    )
    clip_in[pl.ds(local, 1)] = clip_out[pl.ds(local, 1)]
    wait_all(copies)
    summed = clip_in[0].astype(f32)
    for s in range(1, CLIP_DEV):
        summed = summed + clip_in[s].astype(f32)
    grad_ref[...] = summed


def body(
    latents,
    conv_in_weight,
    norm_gain,
    conv_weight,
    frame_list,
    reward_scale,
    patch_weight,
    ln_gain,
    qkv_weight,
    out_weight,
    head_vec,
):
    vmem = pl.BlockSpec(memory_space=pltpu.VMEM)
    smem = pl.BlockSpec(memory_space=pltpu.SMEM)
    anywhere = pl.BlockSpec(memory_space=pl.ANY)
    grad, reward = pl.pallas_call(
        kernel,
        out_shape=(
            jax.ShapeDtypeStruct((16, 128), f32),
            jax.ShapeDtypeStruct((1, 1), f32),
        ),
        in_specs=[vmem, smem, smem, vmem, vmem, vmem, vmem] + [anywhere] * 4,
        out_specs=(vmem, vmem),
        scratch_shapes=[
            pltpu.VMEM((OUT_CH, 27 * CH), bf16),
            pltpu.VMEM((4 * CH, VW), bf16),
            pltpu.VMEM((VW, 3 * HD * LOCAL_HEADS), bf16),
            pltpu.VMEM((HD * LOCAL_HEADS, VW), bf16),
            pltpu.VMEM((640, CH), bf16),
            pltpu.VMEM((2 + CLIP_DEV, 16, 128), bf16),
            pltpu.VMEM((SP, 48, 128), bf16),
            pltpu.VMEM((6, ROWS, 128), f32),
            pltpu.VMEM((8, 15, ROWS, 128), f32),
            pltpu.VMEM((3, COLS, ROWS, 640), bf16),
            pltpu.VMEM((3, COLS, ROWS, CH), bf16),
            pltpu.VMEM((3, 3, COLS + 2, ROWS, CH), bf16),
            pltpu.VMEM((SP, CELLS, OUT_CH), bf16),
            pltpu.VMEM((SP, TOKENS, VW), bf16),
            pltpu.VMEM((3, COLS + 2, ROWS, OUT_CH), bf16),
            pltpu.VMEM((SP, CELLS, OUT_CH), bf16),
            pltpu.VMEM((SP, CELLS, OUT_CH), bf16),
            pltpu.VMEM((7, ROWS, 128), f32),
            pltpu.VMEM((SP, 48, 128), bf16),
            pltpu.VMEM((SP, 48, 128), bf16),
            pltpu.VMEM((15, 16, 128), f32),
            pltpu.VMEM((CLIP_DEV, 16, 128), bf16),
            pltpu.VMEM((CLIP_DEV, 16, 128), bf16),
            pltpu.VMEM((3, COLS, ROWS, 640), f32),
            pltpu.SemaphoreType.DMA((4,)),
            pltpu.SemaphoreType.DMA((4, CLIP_DEV)),
            pltpu.SemaphoreType.DMA((10, SP)),
        ],
        compiler_params=pltpu.CompilerParams(
            collective_id=0, has_side_effects=True, vmem_limit_bytes=48 * 1024 * 1024
        ),
        name="reward_step",
    )(
        latents,
        frame_list,
        reward_scale,
        norm_gain.reshape(1, CH),
        conv_in_weight,
        ln_gain,
        head_vec.reshape(1, VW),
        conv_weight.T,
        patch_weight,
        qkv_weight,
        out_weight,
    )
    spread_rows = grad.reshape(16, 4, 32).transpose(1, 0, 2)
    return (reward.reshape(1), spread_rows.reshape(FR_DEV, ROWS, 32))


def solution(mesh):
    in_specs = (
        P("seq", None, "sp"),
        P(),
        P(),
        P(None, "sp"),
        P(),
        P("seq"),
        P(),
        P(),
        P(None, "sp"),
        P("sp", None),
        P(),
    )
    out_specs = (P("seq"), P("seq", None, "sp"))
    return jax.shard_map(body, mesh=mesh, in_specs=in_specs, out_specs=out_specs, check_vma=False)
```

time: 422 us -> 68.6 us (0.16)
  the two profiles are of different devices: /device:TPU:2 before, /device:TPU:1 now
where the time goes in v1:
time: 68.6 us; the launch traced here: 68.2 us
  Pallas kernels  56 us (82%)
  local copies, waits for them, and re-layouts  9.12 us (13%)
  between operations  3.11 us (5%)
    pallas_call x1, Pallas kernels, body(): pl.pallas_call(kernel, out_shape=(jax.ShapeDtypeStruct((16, 128), f32), j...  56 us
    unnamed x16, local copies, waits for them, and re-layouts  7.73 us

profile of v1, /device:TPU:1, one launch (start us, length us, event | category | flops | bytes accessed | tf_op | source)
XLA Modules:
  0.0 68.2 jit_solution(8875185359733313034)
XLA Ops:
  1.3 0.7 %reshape.19.gain_ref = f32[1,384]{1,0:T(1,128)S(1)} reshape(f32[384]{0:T(512)} %param.13) | data formatting | bytes 3072 | tf_op jit(solution)/shard_map/reshape | solution.py:503
  2.0 0.0 copy-start
  2.0 1.6 %copy-done = bf16[10368,96]{0,1:T(8,128)(2,1)S(1)} copy-done((bf16[10368,96]{0,1:T(8,128)(2,1)S(1)}, bf16[10368,96]{0,1:T(8,128)(2,1)}, u32[]{:S(2)}) %copy-start) | copy-done | bytes 1990680
  3.5 0.0 copy-start.1
  3.5 1.4 %copy-done.1 = bf16[1024,768]{1,0:T(8,128)(2,1)S(1)} copy-done((bf16[1024,768]{1,0:T(8,128)(2,1)S(1)}, bf16[1024,768]{1,0:T(8,128)(2,1)}, u32[]{:S(2)}) %copy-start.1) | copy-done | bytes 1572888
  4.9 0.0 copy-start.2
  4.9 1.0 %copy-done.2 = bf16[256,1024]{1,0:T(8,128)(2,1)S(1)} copy-done((bf16[256,1024]{1,0:T(8,128)(2,1)S(1)}, bf16[256,1024]{1,0:T(8,128)(2,1)}, u32[]{:S(2)}) %copy-start.2) | copy-done | bytes 524312
  6.0 0.0 copy-start.3
  6.0 1.0 %copy-done.3 = bf16[432,384]{1,0:T(8,128)(2,1)S(1)} copy-done((bf16[432,384]{1,0:T(8,128)(2,1)S(1)}, bf16[432,384]{1,0:T(8,128)(2,1)}, u32[]{:S(2)}) %copy-start.3) | copy-done | bytes 331800
  6.9 0.0 copy-start.4
  6.9 0.7 %copy-done.4 = bf16[2,32,32]{2,1,0:T(8,128)(2,1)S(1)} copy-done((bf16[2,32,32]{2,1,0:T(8,128)(2,1)S(1)}, bf16[2,32,32]{2,1,0:T(8,128)(2,1)}, u32[]{:S(2)}) %copy-start.4) | copy-done | bytes 4120
  7.7 0.0 copy-start.5
  7.7 0.7 %copy-done.5 = f32[2,1024]{1,0:T(2,128)S(1)} copy-done((f32[2,1024]{1,0:T(2,128)S(1)}, f32[2,1024]{1,0:T(2,128)}, u32[]{:S(2)}) %copy-start.5) | copy-done | bytes 8216
  8.4 0.0 copy-start.6
  8.4 0.7 %copy-done.6 = f32[1024]{0:T(1024)S(1)} copy-done((f32[1024]{0:T(1024)S(1)}, f32[1024]{0:T(1024)}, u32[]{:S(2)}) %copy-start.6) | copy-done | bytes 4120
  9.0 0.0 copy-start.7
  9.0 0.7 copy-done.7
  9.7 56.0 %reward_step.1 = (f32[16,128]{1,0:T(8,128)S(1)}, f32[1,1]{1,0:T(1,128)}) custom-call(bf16[2,32,32]{2,1,0:T(8,128)(2,1)S(1)} %copy-done.4, s32[64]{0:T(128)S(1)} %copy-done.7, f32[1]{0:T(128)S(6)} %copy.15.scale_ref, f32[1,384]{1,0:T(1,128)S(1)} %reshape.19.gain_ref, bf16[432,384]{1,0:T(8,128)(2,1)S(1)} %copy-done.3, f32[2,1024]{1,0:T(2,128)S(1)} %copy-done.5, ...), custom_call_target="tpu_custom_call" | custom-call | tf_op jit(solution)/shard_map/reward_step/pallas_call | solution.py:458
  65.7 0.1 reshape.22
  65.7 0.6 copy.13
Async XLA Ops:
  2.0 1.6 %copy-start = (bf16[10368,96]{0,1:T(8,128)(2,1)S(1)}, bf16[10368,96]{0,1:T(8,128)(2,1)}, u32[]{:S(2)}) copy-start(bf16[10368,96]{0,1:T(8,128)(2,1)} %param.14) | copy-start | bytes 5971972
  3.5 1.4 %copy-start.1 = (bf16[1024,768]{1,0:T(8,128)(2,1)S(1)}, bf16[1024,768]{1,0:T(8,128)(2,1)}, u32[]{:S(2)}) copy-start(bf16[1024,768]{1,0:T(8,128)(2,1)} %qw_hbm.1) | copy-start | bytes 4718596
  4.9 1.0 %copy-start.2 = (bf16[256,1024]{1,0:T(8,128)(2,1)S(1)}, bf16[256,1024]{1,0:T(8,128)(2,1)}, u32[]{:S(2)}) copy-start(bf16[256,1024]{1,0:T(8,128)(2,1)} %ow_hbm.1) | copy-start | bytes 1572868
  6.0 1.0 %copy-start.3 = (bf16[432,384]{1,0:T(8,128)(2,1)S(1)}, bf16[432,384]{1,0:T(8,128)(2,1)}, u32[]{:S(2)}) copy-start(bf16[432,384]{1,0:T(8,128)(2,1)} %wi_ref.1) | copy-start | bytes 995332
  6.9 0.7 %copy-start.4 = (bf16[2,32,32]{2,1,0:T(8,128)(2,1)S(1)}, bf16[2,32,32]{2,1,0:T(8,128)(2,1)}, u32[]{:S(2)}) copy-start(bf16[2,32,32]{2,1,0:T(8,128)(2,1)} %lat_ref.1) | copy-start | bytes 12292
  7.7 0.7 %copy-start.5 = (f32[2,1024]{1,0:T(2,128)S(1)}, f32[2,1024]{1,0:T(2,128)}, u32[]{:S(2)}) copy-start(f32[2,1024]{1,0:T(2,128)} %ln_ref.1) | copy-start | bytes 24580
  8.4 0.7 %copy-start.6 = (f32[1024]{0:T(1024)S(1)}, f32[1024]{0:T(1024)}, u32[]{:S(2)}) copy-start(f32[1024]{0:T(1024)} %param.21) | copy-start | bytes 12292
  9.0 0.7 copy-start.7

commit v2 on v1

v2 whole, which is shorter than its diff:
```python
import functools

import jax
import jax.numpy as jnp
from jax import lax
from jax.experimental import pallas as pl
from jax.experimental.pallas import tpu as pltpu
from jax.sharding import PartitionSpec as P

LAT = 16
CH = 384
VW = 1024
HD = 64
COLS = 8
ROWS = 32
CLIP_FR = 16
FR_DEV = 2
CLIP_DEV = CLIP_FR // FR_DEV
SP = 4
OUT_CH = CH // SP
LOCAL_HEADS = 4
TOKENS = 64
CELLS = ROWS * COLS
HALF = 64
MESH = pl.DeviceIdType.MESH

norm_epsilon = 1e-06
layer_epsilon = 1e-05

f32 = jnp.float32
bf16 = jnp.bfloat16


def dot(left, right):
    return lax.dot_general(left, right, (((1,), (0,)), ((), ())), preferred_element_type=f32)


def dot_last(left, right):
    return lax.dot_general(left, right, (((1,), (1,)), ((), ())), preferred_element_type=f32)


def dot_first(left, right):
    return lax.dot_general(left, right, (((0,), (0,)), ((), ())), preferred_element_type=f32)


def iota(shape, dim):
    return lax.broadcasted_iota(jnp.int32, shape, dim)


def one_hot(condition):
    return jnp.where(condition, 1.0, 0.0).astype(bf16)


def row_mean(value):
    return jnp.sum(value, axis=-1, keepdims=True) * (1.0 / value.shape[-1])


def layer_stats(volume):
    center = row_mean(volume)
    moved = volume - center
    inverse = lax.rsqrt(row_mean(moved * moved) + layer_epsilon)
    return moved * inverse, inverse


def layer_back(whitened, inverse, scaled_grad):
    return inverse * (
        scaled_grad - row_mean(scaled_grad) - whitened * row_mean(scaled_grad * whitened)
    )


def shifted(value, offset):
    if offset == 0:
        return value
    blank = jnp.zeros(value.shape[:-2] + (1, value.shape[-1]), value.dtype)
    if offset > 0:
        return jnp.concatenate([value[..., 1:, :], blank], axis=-2)
    return jnp.concatenate([blank, value[..., :-1, :]], axis=-2)


def moved(value, offset):
    if offset == 0:
        return value
    blank = jnp.zeros((1,) + value.shape[1:], value.dtype)
    if offset > 0:
        return jnp.concatenate([value[1:], blank], axis=0)
    return jnp.concatenate([blank, value[:-1]], axis=0)


def start_copy(source, target, send, recv, device, pending):
    copy = pltpu.make_async_remote_copy(
        src_ref=source,
        dst_ref=target,
        send_sem=send,
        recv_sem=recv,
        device_id=device,
        device_id_type=MESH,
    )
    copy.start()
    pending.append(copy)
    return copy


def exchange(pick, slots, sems, here, place, count, pending):
    copies = {}
    for step in range(1, count):
        peer = lax.rem(here + step, count)
        copies[step] = start_copy(
            pick(step), slots.at[step], sems.at[0, step], sems.at[1, step], place(peer), pending
        )
    return copies


def wait_all(copies):
    for copy in copies.values():
        copy.wait_recv()


def kernel(
    lat_hbm,
    list_hbm,
    scale_hbm,
    gain_hbm,
    wi_hbm,
    ln_hbm,
    head_hbm,
    conv_hbm,
    patch_hbm,
    qkv_hbm,
    out_hbm,
    grad_ref,
    reward_ref,
    lat_ref,
    list_ref,
    scale_ref,
    gain_ref,
    ln_ref,
    head_ref,
    conv_ref,
    patch_ref,
    qkv_ref,
    out_ref,
    wi_pad,
    lat_seq,
    lat_sp,
    z_ref,
    rolled,
    cols,
    first,
    slope,
    act,
    feat,
    embed,
    mix,
    patch_out,
    patch_in,
    lat_back,
    band_out,
    band_in,
    placed,
    clip_out,
    clip_in,
    back_cols,
    load_sem,
    conv_sem,
    patch_sem,
    seq_sems,
    clip_sems,
    lat_sems,
    feat_sems,
    mix_sems,
    patch_sems,
    band_sems,
    half_sems,
    pair_sems,
):
    seq = lax.axis_index("seq")
    sp = lax.axis_index("sp")
    local = lax.rem(seq, CLIP_DEV)
    base = seq - local

    def in_clip(peer):
        return (base + peer, sp)

    def in_band(peer):
        return (seq, peer)

    loads = {}
    pending = []

    def load(name, source, target, sem):
        copy = pltpu.make_async_copy(source, target, sem)
        copy.start()
        loads.setdefault(name, []).append(copy)

    def loaded(*names):
        for name in names:
            for copy in loads.pop(name):
                copy.wait()

    for i, (name, source, target) in enumerate(
        (
            ("lat", lat_hbm, lat_ref),
            ("list", list_hbm, list_ref),
            ("gain", gain_hbm, gain_ref),
            ("wi", wi_hbm, wi_pad.at[0 : 27 * LAT]),
            ("ln", ln_hbm, ln_ref),
            ("head", head_hbm, head_ref),
            ("scale", scale_hbm, scale_ref),
        )
    ):
        load(name, source, target, load_sem.at[i])

    barrier = pltpu.get_barrier_semaphore()
    for step in range(1, CLIP_DEV):
        pl.semaphore_signal(
            barrier,
            inc=1,
            device_id=in_clip(lax.rem(local + step, CLIP_DEV)),
            device_id_type=MESH,
        )
    for step in range(1, SP):
        pl.semaphore_signal(
            barrier, inc=1, device_id=in_band(lax.rem(sp + step, SP)), device_id_type=MESH
        )

    lat_seq[0:2] = jnp.zeros((2, 16, 128), bf16)
    loaded("lat")
    own = lat_ref[...].reshape(FR_DEV * ROWS, 32)
    packed = jnp.zeros((16, 128), f32)
    for j in range(4):
        spot = one_hot(iota((32, 128), 1) == iota((32, 128), 0) + 32 * j)
        packed = packed + dot(own[16 * j : 16 * j + 16], spot)
    lat_seq[pl.ds(2 + local, 1)] = packed.astype(bf16)[None]

    pl.semaphore_wait(barrier, CLIP_DEV - 1 + SP - 1)

    mine = lat_seq.at[pl.ds(2 + local, 1)]
    copies = {}
    for step in range(1, CLIP_DEV):
        copies[step] = start_copy(
            mine,
            mine,
            seq_sems.at[0, step],
            seq_sems.at[1, step],
            in_clip(lax.rem(local + step, CLIP_DEV)),
            pending,
        )

    half = lax.rem(local, 2)
    out_copies = {}
    for step in range(1, SP):
        out_copies[step] = start_copy(
            out_hbm.at[pl.ds(pl.multiple_of(half * 128, 128), 128)],
            out_ref.at[pl.ds(pl.multiple_of(sp * 256 + half * 128, 128), 128)],
            half_sems.at[0, step],
            half_sems.at[1, step],
            in_band(lax.rem(sp + step, SP)),
            pending,
        )

    for dt in range(3):
        for near in range(9):
            load(
                "conv",
                conv_hbm.at[:, CH * (9 * dt + near) : CH * (9 * dt + near + 1)],
                conv_ref.at[OUT_CH * near : OUT_CH * near + OUT_CH, CH * dt : CH * dt + CH],
                conv_sem.at[dt, near],
            )
    for k in range(4):
        for s in range(SP):
            load(
                "patch",
                patch_hbm.at[CH * k + OUT_CH * s : CH * k + OUT_CH * s + OUT_CH],
                patch_ref.at[CH * s + OUT_CH * k : CH * s + OUT_CH * k + OUT_CH],
                patch_sem.at[k, s],
            )
    load("qkv", qkv_hbm, qkv_ref, load_sem.at[7])
    load("out", out_hbm, out_ref.at[pl.ds(pl.multiple_of(sp * 256, 256), 256)], load_sem.at[8])

    wi_pad[27 * LAT :] = jnp.zeros((512 - 27 * LAT, CH), bf16)
    lat_back[...] = jnp.zeros(lat_back.shape, f32)
    placed[...] = jnp.zeros(placed.shape, f32)
    row, col = iota((512, 512), 0), iota((512, 512), 1)
    swap = one_hot(
        ((row >> 7) == ((col >> 5) & 3)) & (((row >> 5) & 3) == (col >> 7)) & ((row & 31) == (col & 31))
    )
    row, col = iota((256, 256), 0), iota((256, 256), 1)
    kind, token = row >> 6, row & 63
    to_patch = one_hot(
        col == (2 * (token >> 4) + (kind & 1)) * ROWS + 2 * (token & 15) + (kind >> 1)
    )
    own_channels = one_hot(iota((CH, OUT_CH), 0) == iota((CH, OUT_CH), 1) + sp * OUT_CH)

    wait_all(copies)

    loaded("list")
    where = lax.rem(list_ref[seq], CLIP_FR)
    chunk, odd = lax.div(where, 2), lax.rem(where, 2)
    lat_sp[pl.ds(sp, 1)] = lat_seq[pl.ds(chunk, 3)].reshape(1, 48, 128)
    copies = {}
    for step in range(1, SP):
        copies[step] = start_copy(
            lat_sp.at[sp],
            lat_sp.at[sp],
            lat_sems.at[0, step],
            lat_sems.at[1, step],
            in_band(lax.rem(sp + step, SP)),
            pending,
        )
    wait_all(copies)
    wide = jnp.concatenate([lat_sp[s] for s in range(SP)], axis=1)
    spots = dot(wide, swap)
    for c in range(3):
        for j in range(4):
            z_ref[2 * c + j // 2, 16 * (j % 2) : 16 * (j % 2) + 16] = spots[
                16 * c : 16 * c + 16, 128 * j : 128 * j + 128
            ]
    z = z_ref[pl.ds(odd, 5)]
    taps = jnp.stack([shifted(z, dr - 1) for dr in range(3)], axis=1).reshape(480, 128)
    for k in range(8):
        rolled[k] = (taps if k == 0 else pltpu.roll(taps, 16 * k, 1)).reshape(15, ROWS, 128)

    lane = iota((ROWS, 128), 1)
    pieces = []
    for block in range(4):
        inner = lax.rem(lane + 128 * block, 48) >> 4
        taps_here = [t for t in range(9) if 48 * t < 128 * block + 128 and 48 * t + 48 > 128 * block]
        pieces.append((inner, taps_here))

    def inside(inner, c):
        return ((inner > 0) | (c > 0)) & ((inner < 2) | (c < COLS - 1))

    def build(c, carry):
        for frame in range(3):
            for block, (inner, taps_here) in enumerate(pieces):
                value = None
                for tap in taps_here:
                    part = rolled[lax.rem(3 * tap + 9 - c, 8), 3 * frame + tap]
                    begin = 48 * tap - 128 * block
                    value = part if value is None else jnp.where(lane >= begin, part, value)
                cols[frame, c, :, 128 * block : 128 * block + 128] = jnp.where(
                    inside(inner, c), value, 0.0
                ).astype(bf16)
        return carry

    lax.fori_loop(0, COLS, build, 0, unroll=True)

    loaded("gain", "wi")
    gain = gain_ref[...].reshape(1, CH)
    for frame in range(3):
        spots = dot(cols[frame].reshape(CELLS, 512), wi_pad[...])
        first[frame] = spots.astype(bf16)

    for frame in range(3):
        for half_frame in range(2):
            rows = slice(128 * half_frame, 128 * half_frame + 128)
            h = first[frame, rows].astype(f32)
            unit = h * lax.rsqrt(row_mean(h * h) + norm_epsilon) * gain
            act[rows, CH * frame : CH * frame + CH] = (unit * jax.nn.sigmoid(unit)).astype(bf16)

    loaded("conv")
    spots = dot_last(act[...], conv_ref[...])
    total = dot(first[2], own_channels).reshape(COLS, ROWS, OUT_CH)
    for dr in range(3):
        line = None
        for dc in range(3):
            start = OUT_CH * (3 * dr + dc)
            term = moved(spots[:, start : start + OUT_CH].reshape(COLS, ROWS, OUT_CH), dc - 1)
            line = term if line is None else line + term
        total = total + shifted(line, dr - 1)
    patches = dot(to_patch, total.reshape(CELLS, OUT_CH).astype(bf16))
    feat[0] = jnp.concatenate(
        [patches[TOKENS * k : TOKENS * k + TOKENS] for k in range(4)], axis=1
    ).astype(bf16)

    copies = exchange(
        lambda step: feat.at[0], feat, feat_sems, sp, in_band, SP, pending
    )
    loaded("patch")

    def embed_from(step):
        source = lax.rem(sp + SP - step, SP)
        rows = pl.ds(pl.multiple_of(source * CH, 128), CH)
        embed[pl.ds(source, 1)] = dot(feat[step], patch_ref[rows, :])[None]

    embed_from(0)
    for frame in range(3):
        h = first[frame].astype(f32)
        inverse = lax.rsqrt(row_mean(h * h) + norm_epsilon)
        unit = h * inverse * gain
        gate = jax.nn.sigmoid(unit)
        slope[frame] = gate * (1.0 + unit * (1.0 - gate)) * (gain * inverse)
    pair_copies = {}
    for step in range(1, SP):
        out_copies[step].wait_recv()
        source = lax.rem(sp + SP - step, SP)
        got = out_ref.at[pl.ds(pl.multiple_of(source * 256 + half * 128, 128), 128)]
        pair_copies[step] = start_copy(
            got,
            got,
            pair_sems.at[0, step],
            pair_sems.at[1, step],
            (seq + 1 - 2 * half, sp),
            pending,
        )
    for step in (1, 3, 2):
        copies[step].wait_recv()
        embed_from(step)
    loaded("ln", "qkv", "out", "head", "scale")

    x = embed[0]
    for s in range(1, SP):
        x = x + embed[s]
    x = x.astype(bf16).astype(f32)
    white_in, inverse_in = layer_stats(x)
    gain_in, gain_out = ln_ref[0:1], ln_ref[1:2]
    qkv = dot((white_in * gain_in).astype(bf16), qkv_ref[...]).astype(bf16)
    heads = []
    mixed = []
    for head in range(LOCAL_HEADS):
        start = 3 * HD * head
        q, k, v = (qkv[:, start + HD * i : start + HD * i + HD] for i in range(3))
        scores = dot_last(q, k) * (HD**-0.5)
        weights = jnp.exp(scores - jnp.max(scores, axis=-1, keepdims=True))
        probs = weights / jnp.sum(weights, axis=-1, keepdims=True)
        probs_low = probs.astype(bf16)
        mixed.append(dot(probs_low, v).astype(bf16))
        heads.append((q, k, v, probs, probs_low))
    mix[0] = jnp.concatenate(mixed, axis=1)

    copies = exchange(lambda step: mix.at[0], mix, mix_sems, sp, in_band, SP, pending)

    def project_from(step):
        source = lax.rem(sp + SP - step, SP)
        rows = pl.ds(pl.multiple_of(source * 256, 256), 256)
        embed[pl.ds(source, 1)] = dot(mix[step], out_ref[rows, :])[None]

    project_from(0)
    wait_all(pair_copies)
    for step in (1, 3, 2):
        copies[step].wait_recv()
        project_from(step)

    attended = embed[0]
    for s in range(1, SP):
        attended = attended + embed[s]
    y = x + attended
    white_out, inverse_out = layer_stats(y)
    vector = head_ref[...].reshape(1, VW)
    reward = jnp.sum(white_out * gain_out * vector, axis=1, keepdims=True)
    reward_ref[...] = jnp.sum(reward, axis=0, keepdims=True) * (1.0 / TOKENS)
    scaled = (scale_ref[0] * (1.0 / TOKENS)) * vector * gain_out
    dy = layer_back(white_out, inverse_out, jnp.broadcast_to(scaled, y.shape))
    own_out = out_ref[pl.ds(pl.multiple_of(sp * 256, 256), 256), :]
    do = dot_last(dy.astype(bf16), own_out).astype(bf16)
    grads = []
    for head in range(LOCAL_HEADS):
        q, k, v, probs, probs_low = heads[head]
        d_out = do[:, HD * head : HD * head + HD]
        d_probs = dot_last(d_out, v)
        d_scores = (
            probs
            * (d_probs - jnp.sum(d_probs * probs, axis=-1, keepdims=True))
            * (HD**-0.5)
        ).astype(bf16)
        grads.append(dot(d_scores, k).astype(bf16))
        grads.append(dot_first(d_scores, q).astype(bf16))
        grads.append(dot_first(probs_low, d_out).astype(bf16))
    da = dot_last(jnp.concatenate(grads, axis=1), qkv_ref[...])
    dx = layer_back(white_in, inverse_in, da * gain_in) + dy * (1.0 / SP)
    dx_low = dx.astype(bf16)
    copies = {}
    for step in (2, 1, 3, 0):
        peer = lax.rem(sp + step, SP)
        rows = pl.ds(pl.multiple_of(peer * CH, 128), CH)
        block = dot_last(dx_low, patch_ref[rows, :]).astype(bf16)
        if step == 0:
            patch_in[0] = block
        else:
            patch_out[step] = block
            copies[step] = start_copy(
                patch_out.at[step],
                patch_in.at[step],
                patch_sems.at[0, step],
                patch_sems.at[1, step],
                in_band(peer),
                pending,
            )

    wait_all(copies)

    summed = patch_in[0].astype(f32)
    for s in range(1, SP):
        summed = summed + patch_in[s].astype(f32)
    summed = jnp.concatenate(
        [summed[:, OUT_CH * k : OUT_CH * k + OUT_CH] for k in range(4)], axis=0
    )
    d_feat = dot_first(to_patch, summed.astype(bf16))
    d_cells = d_feat.reshape(COLS, ROWS, OUT_CH)
    lines = [shifted(d_cells, 1 - dr).astype(bf16) for dr in range(3)]
    spread_out = jnp.concatenate(
        [
            moved(lines[dr], 1 - dc).reshape(CELLS, OUT_CH)
            for dr in range(3)
            for dc in range(3)
        ],
        axis=1,
    )
    d_own = dot_last(d_feat.astype(bf16), own_channels)

    for frame in (2, 1, 0):
        d_act = dot(spread_out, conv_ref[:, CH * frame : CH * frame + CH])
        h = first[frame].astype(f32)
        square = row_mean(h * h) + norm_epsilon
        d_unit = d_act * slope[frame]
        d_first = d_unit - h * (row_mean(d_unit * h) / square)
        if frame == 2:
            d_first = d_first + d_own
        back_cols[frame] = dot_last(d_first.astype(bf16), wi_pad[...]).reshape(COLS, ROWS, 512)

    def collect(c, carry):
        totals = list(carry)
        for frame in range(3):
            for block, (inner, taps_here) in enumerate(pieces):
                value = jnp.where(
                    inside(inner, c), back_cols[frame, c, :, 128 * block : 128 * block + 128], 0.0
                )
                for tap in taps_here:
                    begin = 48 * tap - 128 * block
                    within = value
                    if begin > 0:
                        within = jnp.where(lane >= begin, within, 0.0)
                    if begin + 48 < 128:
                        within = jnp.where(lane < begin + 48, within, 0.0)
                    turn = lax.rem(16 * (c + 23 - 3 * tap + 8), 128)
                    totals[3 * frame + tap] = totals[3 * frame + tap] + pltpu.roll(within, turn, 1)
        return tuple(totals)

    gathered = lax.fori_loop(
        0, COLS, collect, tuple(jnp.zeros((ROWS, 128), f32) for _ in range(15)), unroll=True
    )
    gathered = jnp.stack(gathered, axis=0)
    gathered = gathered.reshape(5, 3, ROWS, 128)
    lat_back[1:6] = (
        gathered[:, 1] + shifted(gathered[:, 0], 1) + shifted(gathered[:, 2], -1)
    )
    aligned = lat_back[pl.ds(1 - odd, 6)].astype(bf16)
    wide = jnp.concatenate(
        [
            jnp.concatenate(
                [aligned[2 * c + j // 2, 16 * (j % 2) : 16 * (j % 2) + 16] for j in range(4)], axis=1
            )
            for c in range(3)
        ],
        axis=0,
    )
    bands = dot(wide, swap).astype(bf16)
    for s in range(SP):
        band_out[s] = bands[:, 128 * s : 128 * s + 128]

    copies = exchange(
        lambda step: band_out.at[lax.rem(sp + step, SP)],
        band_in,
        band_sems,
        sp,
        in_band,
        SP,
        pending,
    )
    band_in[pl.ds(0, 1)] = band_out[pl.ds(sp, 1)]
    wait_all(copies)

    summed = band_in[0].astype(f32)
    for s in range(1, SP):
        summed = summed + band_in[s].astype(f32)
    placed[5:8] = summed.reshape(3, 16, 128)
    clip_out[...] = placed[pl.ds(7 - chunk, 8)].astype(bf16)
    copies = exchange(
        lambda step: clip_out.at[lax.rem(local + step, CLIP_DEV)],
        clip_in,
        clip_sems,
        local,
        in_clip,
        CLIP_DEV,
        pending,
    )
    clip_in[pl.ds(0, 1)] = clip_out[pl.ds(local, 1)]
    wait_all(copies)

    summed = clip_in[0].astype(f32)
    for s in range(1, CLIP_DEV):
        summed = summed + clip_in[s].astype(f32)
    grad_ref[...] = summed
    for copy in pending:
        copy.wait_send()


def body(
    latents,
    conv_in_weight,
    norm_gain,
    conv_weight,
    frame_list,
    reward_scale,
    patch_weight,
    ln_gain,
    qkv_weight,
    out_weight,
    head_vec,
):
    vmem = pl.BlockSpec(memory_space=pltpu.VMEM)
    hbm = pl.BlockSpec(memory_space=pltpu.HBM)
    grad, reward = pl.pallas_call(
        kernel,
        out_shape=(
            jax.ShapeDtypeStruct((16, 128), f32),
            jax.ShapeDtypeStruct((1, 1), f32),
        ),
        in_specs=[hbm] * 11,
        out_specs=(vmem, vmem),
        scratch_shapes=[
            pltpu.VMEM((FR_DEV, ROWS, 32), bf16),
            pltpu.SMEM((64,), jnp.int32),
            pltpu.SMEM((1,), f32),
            pltpu.VMEM((CH,), f32),
            pltpu.VMEM((2, VW), f32),
            pltpu.VMEM((VW,), f32),
            pltpu.VMEM((9 * OUT_CH, 3 * CH), bf16),
            pltpu.VMEM((4 * CH, VW), bf16),
            pltpu.VMEM((VW, 3 * HD * LOCAL_HEADS), bf16),
            pltpu.VMEM((VW, VW), bf16),
            pltpu.VMEM((512, CH), bf16),
            pltpu.VMEM((2 + CLIP_DEV, 16, 128), bf16),
            pltpu.VMEM((SP, 48, 128), bf16),
            pltpu.VMEM((6, ROWS, 128), f32),
            pltpu.VMEM((8, 15, ROWS, 128), f32),
            pltpu.VMEM((3, COLS, ROWS, 512), bf16),
            pltpu.VMEM((3, CELLS, CH), bf16),
            pltpu.VMEM((3, CELLS, CH), f32),
            pltpu.VMEM((CELLS, 3 * CH), bf16),
            pltpu.VMEM((SP, TOKENS, CH), bf16),
            pltpu.VMEM((SP, TOKENS, VW), f32),
            pltpu.VMEM((SP, TOKENS, HD * LOCAL_HEADS), bf16),
            pltpu.VMEM((SP, TOKENS, CH), bf16),
            pltpu.VMEM((SP, TOKENS, CH), bf16),
            pltpu.VMEM((7, ROWS, 128), f32),
            pltpu.VMEM((SP, 48, 128), bf16),
            pltpu.VMEM((SP, 48, 128), bf16),
            pltpu.VMEM((15, 16, 128), f32),
            pltpu.VMEM((CLIP_DEV, 16, 128), bf16),
            pltpu.VMEM((CLIP_DEV, 16, 128), bf16),
            pltpu.VMEM((3, COLS, ROWS, 512), f32),
            pltpu.SemaphoreType.DMA((9,)),
            pltpu.SemaphoreType.DMA((3, 9)),
            pltpu.SemaphoreType.DMA((4, SP)),
            pltpu.SemaphoreType.DMA((2, CLIP_DEV)),
            pltpu.SemaphoreType.DMA((2, CLIP_DEV)),
        ]
        + [pltpu.SemaphoreType.DMA((2, SP))] * 7,
        compiler_params=pltpu.CompilerParams(
            collective_id=0, has_side_effects=True, vmem_limit_bytes=60 * 1024 * 1024
        ),
        name="reward_step",
    )(
        latents,
        frame_list,
        reward_scale,
        norm_gain,
        conv_in_weight,
        ln_gain,
        head_vec,
        conv_weight.T,
        patch_weight,
        qkv_weight,
        out_weight,
    )
    spread_rows = grad.reshape(16, 4, 32).transpose(1, 0, 2)
    return (reward.reshape(1), spread_rows.reshape(FR_DEV, ROWS, 32))


def solution(mesh):
    in_specs = (
        P("seq", None, "sp"),
        P(),
        P(),
        P(None, "sp"),
        P(),
        P("seq"),
        P(),
        P(),
        P(None, "sp"),
        P("sp", None),
        P(),
    )
    out_specs = (P("seq"), P("seq", None, "sp"))
    return jax.shard_map(body, mesh=mesh, in_specs=in_specs, out_specs=out_specs, check_vma=False)
```

time: 68.6 us -> 58.5 us (0.85)
  local copies, waits for them, and re-layouts: 9.12 us -> 1.4 us
  Pallas kernels: 56 us -> 53.8 us
    unnamed x16 -> x0, local copies, waits for them, and re-layouts: 7.73 us -> none
    pallas_call x1, Pallas kernels: 56 us -> 53.8 us  [body(): pl.pallas_call(kernel, out_shape=(jax.ShapeDtypeStruct((16, 128), f32), j...]
    reshape x1, local copies, waits for them, and re-layouts: 0.08 us -> 0.78 us  [body(): spread_rows = grad.reshape(16, 4, 32).transpose(1, 0, 2)]
where the time goes in v2:
time: 58.5 us; the launch traced here: 58.2 us
  Pallas kernels  53.8 us (92%)
  between operations  3.05 us (5%)
  local copies, waits for them, and re-layouts  1.4 us (2%)
    pallas_call x1, Pallas kernels, body(): pl.pallas_call(kernel, out_shape=(jax.ShapeDtypeStruct((16, 128), f32), j...  53.8 us

profile of v2, /device:TPU:1, one launch (start us, length us, event | category | flops | bytes accessed | tf_op | source)
XLA Modules:
  0.0 58.2 jit_solution(15736350194399621233)
XLA Ops:
  1.3 53.8 %reward_step.1 = (f32[16,128]{1,0:T(8,128)}, f32[1,1]{1,0:T(1,128)}) custom-call(bf16[2,32,32]{2,1,0:T(8,128)(2,1)} %lat_hbm.1, s32[64]{0:T(128)} %list_hbm.1, f32[1]{0:T(128)S(6)} %copy.15.scale_hbm, f32[384]{0:T(512)} %gain_hbm.1, bf16[432,384]{1,0:T(8,128)(2,1)} %wi_hbm.1, f32[2,1024]{1,0:T(2,128)} %ln_hbm.1, f32[1024]{0:T(1024)} %head_hbm.1, ...), custom_call_target="tpu_custom_call" | custom-call | tf_op jit(solution)/shard_map/reward_step/pallas_call | solution.py:613
  55.1 0.8 %reshape.14 = f32[16,4,32]{2,1,0:T(4,128)S(1)} reshape(f32[16,128]{1,0:T(8,128)} %get-tuple-element.5) | data formatting | bytes 16384 | tf_op jit(solution)/shard_map/reshape | solution.py:677
  55.9 0.6 %copy.13 = f32[4,16,32]{2,1,0:T(8,128)} copy(f32[4,16,32]{2,0,1:T(4,128)S(1)} %bitcast.5) | data formatting | bytes 16384 | tf_op jit(solution)/shard_map/transpose | solution.py:677

commit v3 on v2

--- a/solution.py
+++ b/solution.py
@@ -170,8 +170,6 @@
     mix_sems,
     patch_sems,
     band_sems,
-    half_sems,
-    pair_sems,
 ):
     seq = lax.axis_index("seq")
     sp = lax.axis_index("sp")
@@ -243,18 +241,6 @@
             seq_sems.at[0, step],
             seq_sems.at[1, step],
             in_clip(lax.rem(local + step, CLIP_DEV)),
-            pending,
-        )
-
-    half = lax.rem(local, 2)
-    out_copies = {}
-    for step in range(1, SP):
-        out_copies[step] = start_copy(
-            out_hbm.at[pl.ds(pl.multiple_of(half * 128, 128), 128)],
-            out_ref.at[pl.ds(pl.multiple_of(sp * 256 + half * 128, 128), 128)],
-            half_sems.at[0, step],
-            half_sems.at[1, step],
-            in_band(lax.rem(sp + step, SP)),
             pending,
         )
 
@@ -275,7 +261,7 @@
                 patch_sem.at[k, s],
             )
     load("qkv", qkv_hbm, qkv_ref, load_sem.at[7])
-    load("out", out_hbm, out_ref.at[pl.ds(pl.multiple_of(sp * 256, 256), 256)], load_sem.at[8])
+    load("out", out_hbm, out_ref, load_sem.at[8])
 
     wi_pad[27 * LAT :] = jnp.zeros((512 - 27 * LAT, CH), bf16)
     lat_back[...] = jnp.zeros(lat_back.shape, f32)
@@ -390,19 +376,6 @@
         unit = h * inverse * gain
         gate = jax.nn.sigmoid(unit)
         slope[frame] = gate * (1.0 + unit * (1.0 - gate)) * (gain * inverse)
-    pair_copies = {}
-    for step in range(1, SP):
-        out_copies[step].wait_recv()
-        source = lax.rem(sp + SP - step, SP)
-        got = out_ref.at[pl.ds(pl.multiple_of(source * 256 + half * 128, 128), 128)]
-        pair_copies[step] = start_copy(
-            got,
-            got,
-            pair_sems.at[0, step],
-            pair_sems.at[1, step],
-            (seq + 1 - 2 * half, sp),
-            pending,
-        )
     for step in (1, 3, 2):
         copies[step].wait_recv()
         embed_from(step)
@@ -426,24 +399,23 @@
         probs_low = probs.astype(bf16)
         mixed.append(dot(probs_low, v).astype(bf16))
         heads.append((q, k, v, probs, probs_low))
-    mix[0] = jnp.concatenate(mixed, axis=1)
-
-    copies = exchange(lambda step: mix.at[0], mix, mix_sems, sp, in_band, SP, pending)
-
-    def project_from(step):
-        source = lax.rem(sp + SP - step, SP)
-        rows = pl.ds(pl.multiple_of(source * 256, 256), 256)
-        embed[pl.ds(source, 1)] = dot(mix[step], out_ref[rows, :])[None]
-
-    project_from(0)
-    wait_all(pair_copies)
-    for step in (1, 3, 2):
-        copies[step].wait_recv()
-        project_from(step)
-
-    attended = embed[0]
+    mix[pl.ds(sp, 1)] = dot(jnp.concatenate(mixed, axis=1), out_ref[...]).astype(bf16)[None]
+
+    copies = {}
+    for step in range(1, SP):
+        copies[step] = start_copy(
+            mix.at[sp],
+            mix.at[sp],
+            mix_sems.at[0, step],
+            mix_sems.at[1, step],
+            in_band(lax.rem(sp + step, SP)),
+            pending,
+        )
+    wait_all(copies)
+
+    attended = mix[0].astype(f32)
     for s in range(1, SP):
-        attended = attended + embed[s]
+        attended = attended + mix[s].astype(f32)
     y = x + attended
     white_out, inverse_out = layer_stats(y)
     vector = head_ref[...].reshape(1, VW)
@@ -451,8 +423,7 @@
     reward_ref[...] = jnp.sum(reward, axis=0, keepdims=True) * (1.0 / TOKENS)
     scaled = (scale_ref[0] * (1.0 / TOKENS)) * vector * gain_out
     dy = layer_back(white_out, inverse_out, jnp.broadcast_to(scaled, y.shape))
-    own_out = out_ref[pl.ds(pl.multiple_of(sp * 256, 256), 256), :]
-    do = dot_last(dy.astype(bf16), own_out).astype(bf16)
+    do = dot_last(dy.astype(bf16), out_ref[...]).astype(bf16)
     grads = []
     for head in range(LOCAL_HEADS):
         q, k, v, probs, probs_low = heads[head]
@@ -590,7 +561,8 @@
     summed = clip_in[0].astype(f32)
     for s in range(1, CLIP_DEV):
         summed = summed + clip_in[s].astype(f32)
-    grad_ref[...] = summed
+    for j in range(4):
+        grad_ref[j // 2, 16 * (j % 2) : 16 * (j % 2) + 16] = summed[:, 32 * j : 32 * j + 32]
     for copy in pending:
         copy.wait_send()
 
@@ -613,7 +585,7 @@
     grad, reward = pl.pallas_call(
         kernel,
         out_shape=(
-            jax.ShapeDtypeStruct((16, 128), f32),
+            jax.ShapeDtypeStruct((FR_DEV, ROWS, 32), f32),
             jax.ShapeDtypeStruct((1, 1), f32),
         ),
         in_specs=[hbm] * 11,
@@ -628,7 +600,7 @@
             pltpu.VMEM((9 * OUT_CH, 3 * CH), bf16),
             pltpu.VMEM((4 * CH, VW), bf16),
             pltpu.VMEM((VW, 3 * HD * LOCAL_HEADS), bf16),
-            pltpu.VMEM((VW, VW), bf16),
+            pltpu.VMEM((HD * LOCAL_HEADS, VW), bf16),
             pltpu.VMEM((512, CH), bf16),
             pltpu.VMEM((2 + CLIP_DEV, 16, 128), bf16),
             pltpu.VMEM((SP, 48, 128), bf16),
@@ -640,7 +612,7 @@
             pltpu.VMEM((CELLS, 3 * CH), bf16),
             pltpu.VMEM((SP, TOKENS, CH), bf16),
             pltpu.VMEM((SP, TOKENS, VW), f32),
-            pltpu.VMEM((SP, TOKENS, HD * LOCAL_HEADS), bf16),
+            pltpu.VMEM((SP, TOKENS, VW), bf16),
             pltpu.VMEM((SP, TOKENS, CH), bf16),
             pltpu.VMEM((SP, TOKENS, CH), bf16),
             pltpu.VMEM((7, ROWS, 128), f32),
@@ -656,7 +628,7 @@
             pltpu.SemaphoreType.DMA((2, CLIP_DEV)),
             pltpu.SemaphoreType.DMA((2, CLIP_DEV)),
         ]
-        + [pltpu.SemaphoreType.DMA((2, SP))] * 7,
+        + [pltpu.SemaphoreType.DMA((2, SP))] * 5,
         compiler_params=pltpu.CompilerParams(
             collective_id=0, has_side_effects=True, vmem_limit_bytes=60 * 1024 * 1024
         ),
@@ -674,8 +646,7 @@
         qkv_weight,
         out_weight,
     )
-    spread_rows = grad.reshape(16, 4, 32).transpose(1, 0, 2)
-    return (reward.reshape(1), spread_rows.reshape(FR_DEV, ROWS, 32))
+    return (reward.reshape(1), grad)
 
 
 def solution(mesh):

time: 58.5 us -> 54.2 us (0.926)
  Pallas kernels: 53.8 us -> 49.6 us
    pallas_call x1, Pallas kernels: 53.8 us -> 49.6 us  [body(): pl.pallas_call(kernel, out_shape=(jax.ShapeDtypeStruct((FR_DEV, ROWS, 32)...]
    unnamed x0 -> x1, local copies, waits for them, and re-layouts: none -> 1.38 us
    reshape x1 -> x0, local copies, waits for them, and re-layouts: 0.78 us -> none  [body(): spread_rows = grad.reshape(16, 4, 32).transpose(1, 0, 2)]
    transpose x1 -> x0, local copies, waits for them, and re-layouts: 0.62 us -> none  [body(): spread_rows = grad.reshape(16, 4, 32).transpose(1, 0, 2)]
where the time goes in v3:
time: 54.2 us; the launch traced here: 54.1 us
  Pallas kernels  49.6 us (92%)
  between operations  3.05 us (6%)
  local copies, waits for them, and re-layouts  1.38 us (3%)
    pallas_call x1, Pallas kernels, body(): pl.pallas_call(kernel, out_shape=(jax.ShapeDtypeStruct((FR_DEV, ROWS, 32)...  49.6 us
    unnamed x1, local copies, waits for them, and re-layouts  1.38 us

profile of v3, /device:TPU:1, one launch (start us, length us, event | category | flops | bytes accessed | tf_op | source)
XLA Modules:
  0.0 54.1 jit_solution(5210924661911493078)
XLA Ops:
  1.3 49.6 %reward_step.1 = (f32[2,32,32]{2,1,0:T(8,128)}, f32[1,1]{1,0:T(1,128)}) custom-call(bf16[2,32,32]{2,1,0:T(8,128)(2,1)} %lat_hbm.1, s32[64]{0:T(128)} %list_hbm.1, f32[1]{0:T(128)S(6)} %copy.15.scale_hbm, f32[384]{0:T(512)} %gain_hbm.1, bf16[432,384]{1,0:T(8,128)(2,1)} %wi_hbm.1, f32[2,1024]{1,0:T(2,128)} %ln_hbm.1, f32[1024]{0:T(1024)} %head_hbm.1, ...), custom_call_target="tpu_custom_call" | custom-call | tf_op jit(solution)/shard_map/reward_step/pallas_call | solution.py:585
  51.5 1.4 %copy.17 = f32[2,32,32]{2,1,0:T(8,128)} copy(f32[2,32,32]{2,1,0:T(8,128)} %get-tuple-element.9) | data formatting | bytes 16384

commit v4 on v3

--- a/solution.py
+++ b/solution.py
@@ -102,7 +102,7 @@
 
 def exchange(pick, slots, sems, here, place, count, pending):
     copies = {}
-    for step in range(1, count):
+    for step in sorted(range(1, count), key=lambda d: -min(d, count - d)):
         peer = lax.rem(here + step, count)
         copies[step] = start_copy(
             pick(step), slots.at[step], sems.at[0, step], sems.at[1, step], place(peer), pending
@@ -127,8 +127,8 @@
     patch_hbm,
     qkv_hbm,
     out_hbm,
-    grad_ref,
-    reward_ref,
+    clip_in,
+    reward_hbm,
     lat_ref,
     list_ref,
     scale_ref,
@@ -158,7 +158,7 @@
     band_in,
     placed,
     clip_out,
-    clip_in,
+    reward_ref,
     back_cols,
     load_sem,
     conv_sem,
@@ -182,6 +182,19 @@
     def in_band(peer):
         return (seq, peer)
 
+    barrier = pltpu.get_barrier_semaphore()
+    for step in range(1, CLIP_DEV):
+        pl.semaphore_signal(
+            barrier,
+            inc=1,
+            device_id=in_clip(lax.rem(local + step, CLIP_DEV)),
+            device_id_type=MESH,
+        )
+    for step in range(1, SP):
+        pl.semaphore_signal(
+            barrier, inc=1, device_id=in_band(lax.rem(sp + step, SP)), device_id_type=MESH
+        )
+
     loads = {}
     pending = []
 
@@ -207,19 +220,6 @@
         )
     ):
         load(name, source, target, load_sem.at[i])
-
-    barrier = pltpu.get_barrier_semaphore()
-    for step in range(1, CLIP_DEV):
-        pl.semaphore_signal(
-            barrier,
-            inc=1,
-            device_id=in_clip(lax.rem(local + step, CLIP_DEV)),
-            device_id_type=MESH,
-        )
-    for step in range(1, SP):
-        pl.semaphore_signal(
-            barrier, inc=1, device_id=in_band(lax.rem(sp + step, SP)), device_id_type=MESH
-        )
 
     lat_seq[0:2] = jnp.zeros((2, 16, 128), bf16)
     loaded("lat")
@@ -284,7 +284,7 @@
     chunk, odd = lax.div(where, 2), lax.rem(where, 2)
     lat_sp[pl.ds(sp, 1)] = lat_seq[pl.ds(chunk, 3)].reshape(1, 48, 128)
     copies = {}
-    for step in range(1, SP):
+    for step in (2, 1, 3):
         copies[step] = start_copy(
             lat_sp.at[sp],
             lat_sp.at[sp],
@@ -388,21 +388,24 @@
     white_in, inverse_in = layer_stats(x)
     gain_in, gain_out = ln_ref[0:1], ln_ref[1:2]
     qkv = dot((white_in * gain_in).astype(bf16), qkv_ref[...]).astype(bf16)
-    heads = []
-    mixed = []
-    for head in range(LOCAL_HEADS):
-        start = 3 * HD * head
-        q, k, v = (qkv[:, start + HD * i : start + HD * i + HD] for i in range(3))
-        scores = dot_last(q, k) * (HD**-0.5)
-        weights = jnp.exp(scores - jnp.max(scores, axis=-1, keepdims=True))
-        probs = weights / jnp.sum(weights, axis=-1, keepdims=True)
-        probs_low = probs.astype(bf16)
-        mixed.append(dot(probs_low, v).astype(bf16))
-        heads.append((q, k, v, probs, probs_low))
+    heads = range(LOCAL_HEADS)
+
+    def part_of(i):
+        return [qkv[:, HD * (3 * h + i) : HD * (3 * h + i) + HD] for h in heads]
+
+    def rows_of(stacked):
+        return [stacked[TOKENS * h : TOKENS * h + TOKENS] for h in heads]
+
+    query, key, value = part_of(0), part_of(1), part_of(2)
+    scores = jnp.concatenate([dot_last(query[h], key[h]) for h in heads], axis=0) * (HD**-0.5)
+    weights = jnp.exp(scores - jnp.max(scores, axis=-1, keepdims=True))
+    probs = weights / jnp.sum(weights, axis=-1, keepdims=True)
+    probs_low = rows_of(probs.astype(bf16))
+    mixed = [dot(probs_low[h], value[h]).astype(bf16) for h in heads]
     mix[pl.ds(sp, 1)] = dot(jnp.concatenate(mixed, axis=1), out_ref[...]).astype(bf16)[None]
 
     copies = {}
-    for step in range(1, SP):
+    for step in (2, 1, 3):
         copies[step] = start_copy(
             mix.at[sp],
             mix.at[sp],
@@ -420,23 +423,22 @@
     white_out, inverse_out = layer_stats(y)
     vector = head_ref[...].reshape(1, VW)
     reward = jnp.sum(white_out * gain_out * vector, axis=1, keepdims=True)
-    reward_ref[...] = jnp.sum(reward, axis=0, keepdims=True) * (1.0 / TOKENS)
+    reward_ref[...] = jnp.broadcast_to(
+        jnp.sum(reward, axis=0, keepdims=True) * (1.0 / TOKENS), (8, 128)
+    )
+    load("reward", reward_ref, reward_hbm, load_sem.at[9])
     scaled = (scale_ref[0] * (1.0 / TOKENS)) * vector * gain_out
     dy = layer_back(white_out, inverse_out, jnp.broadcast_to(scaled, y.shape))
     do = dot_last(dy.astype(bf16), out_ref[...]).astype(bf16)
+    d_out = [do[:, HD * h : HD * h + HD] for h in heads]
+    d_probs = jnp.concatenate([dot_last(d_out[h], value[h]) for h in heads], axis=0)
+    d_scores = probs * (d_probs - jnp.sum(d_probs * probs, axis=-1, keepdims=True)) * (HD**-0.5)
+    d_scores = rows_of(d_scores.astype(bf16))
     grads = []
-    for head in range(LOCAL_HEADS):
-        q, k, v, probs, probs_low = heads[head]
-        d_out = do[:, HD * head : HD * head + HD]
-        d_probs = dot_last(d_out, v)
-        d_scores = (
-            probs
-            * (d_probs - jnp.sum(d_probs * probs, axis=-1, keepdims=True))
-            * (HD**-0.5)
-        ).astype(bf16)
-        grads.append(dot(d_scores, k).astype(bf16))
-        grads.append(dot_first(d_scores, q).astype(bf16))
-        grads.append(dot_first(probs_low, d_out).astype(bf16))
+    for h in heads:
+        grads.append(dot(d_scores[h], key[h]).astype(bf16))
+        grads.append(dot_first(d_scores[h], query[h]).astype(bf16))
+        grads.append(dot_first(probs_low[h], d_out[h]).astype(bf16))
     da = dot_last(jnp.concatenate(grads, axis=1), qkv_ref[...])
     dx = layer_back(white_in, inverse_in, da * gain_in) + dy * (1.0 / SP)
     dx_low = dx.astype(bf16)
@@ -555,16 +557,21 @@
         CLIP_DEV,
         pending,
     )
-    clip_in[pl.ds(0, 1)] = clip_out[pl.ds(local, 1)]
+    load("clip", clip_out.at[pl.ds(local, 1)], clip_in.at[0:1], load_sem.at[10])
     wait_all(copies)
 
+    loaded("clip", "reward")
+    for copy in pending:
+        copy.wait_send()
+
+
+def finish(clip_in, reward_in, reward_ref, grad_ref):
     summed = clip_in[0].astype(f32)
     for s in range(1, CLIP_DEV):
         summed = summed + clip_in[s].astype(f32)
     for j in range(4):
         grad_ref[j // 2, 16 * (j % 2) : 16 * (j % 2) + 16] = summed[:, 32 * j : 32 * j + 32]
-    for copy in pending:
-        copy.wait_send()
+    reward_ref[...] = reward_in[0:1, 0:1]
 
 
 def body(
@@ -582,14 +589,14 @@
 ):
     vmem = pl.BlockSpec(memory_space=pltpu.VMEM)
     hbm = pl.BlockSpec(memory_space=pltpu.HBM)
-    grad, reward = pl.pallas_call(
+    parts, rewards = pl.pallas_call(
         kernel,
         out_shape=(
-            jax.ShapeDtypeStruct((FR_DEV, ROWS, 32), f32),
-            jax.ShapeDtypeStruct((1, 1), f32),
+            jax.ShapeDtypeStruct((CLIP_DEV, 16, 128), bf16),
+            jax.ShapeDtypeStruct((8, 128), f32),
         ),
         in_specs=[hbm] * 11,
-        out_specs=(vmem, vmem),
+        out_specs=(hbm, hbm),
         scratch_shapes=[
             pltpu.VMEM((FR_DEV, ROWS, 32), bf16),
             pltpu.SMEM((64,), jnp.int32),
@@ -620,9 +627,9 @@
             pltpu.VMEM((SP, 48, 128), bf16),
             pltpu.VMEM((15, 16, 128), f32),
             pltpu.VMEM((CLIP_DEV, 16, 128), bf16),
-            pltpu.VMEM((CLIP_DEV, 16, 128), bf16),
+            pltpu.VMEM((8, 128), f32),
             pltpu.VMEM((3, COLS, ROWS, 512), f32),
-            pltpu.SemaphoreType.DMA((9,)),
+            pltpu.SemaphoreType.DMA((11,)),
             pltpu.SemaphoreType.DMA((3, 9)),
             pltpu.SemaphoreType.DMA((4, SP)),
             pltpu.SemaphoreType.DMA((2, CLIP_DEV)),
@@ -646,6 +653,16 @@
         qkv_weight,
         out_weight,
     )
+    reward, grad = pl.pallas_call(
+        finish,
+        out_shape=(
+            jax.ShapeDtypeStruct((1, 1), f32),
+            jax.ShapeDtypeStruct((FR_DEV, ROWS, 32), f32),
+        ),
+        in_specs=[vmem, vmem],
+        out_specs=(vmem, vmem),
+        name="finish",
+    )(parts, rewards)
     return (reward.reshape(1), grad)
 
 

time: 54.2 us -> 49.7 us (0.917)
  between operations: 3.05 us -> 1.29 us
  Pallas kernels: 49.6 us -> 48.2 us
  local copies, waits for them, and re-layouts: 1.38 us -> 0 us
    pallas_call x1 -> x2, Pallas kernels: 49.6 us -> 48.2 us  [the longest x1 46.8 us: body(): pl.pallas_call(kernel, out_shape=(jax.ShapeDtypeStruct((CLIP_DEV, 16, 128...]
    unnamed x1 -> x0, local copies, waits for them, and re-layouts: 1.38 us -> none
where the time goes in v4:
time: 49.7 us; the launch traced here: 49.5 us
  Pallas kernels  48.2 us (97%)
  between operations  1.29 us (3%)
    pallas_call x1, Pallas kernels, body(): pl.pallas_call(kernel, out_shape=(jax.ShapeDtypeStruct((CLIP_DEV, 16, 128...  46.8 us
    pallas_call x1, Pallas kernels, body(): pl.pallas_call(finish, out_shape=(jax.ShapeDtypeStruct((1, 1), f32), jax....  1.46 us

profile of v4, /device:TPU:1, one launch (start us, length us, event | category | flops | bytes accessed | tf_op | source)
XLA Modules:
  0.0 49.5 jit_solution(1682397760324156030)
XLA Ops:
  1.3 46.8 %reward_step.1 = (bf16[8,16,128]{2,1,0:T(8,128)(2,1)}, f32[8,128]{1,0:T(8,128)}) custom-call(bf16[2,32,32]{2,1,0:T(8,128)(2,1)} %lat_hbm.1, s32[64]{0:T(128)} %list_hbm.1, f32[1]{0:T(128)S(6)} %copy.13.scale_hbm, f32[384]{0:T(512)} %gain_hbm.1, bf16[432,384]{1,0:T(8,128)(2,1)} %wi_hbm.1, f32[2,1024]{1,0:T(2,128)} %ln_hbm.1, f32[1024]{0:T(1024)} %head_hbm.1, ...), custom_call_target="tpu_custom_call" | custom-call | tf_op jit(solution)/shard_map/reward_step/pallas_call | solution.py:592
  48.1 1.5 %finish.1 = (f32[1,1]{1,0:T(1,128)}, f32[2,32,32]{2,1,0:T(8,128)}) custom-call(bf16[8,16,128]{2,1,0:T(8,128)(2,1)} %get-tuple-element.6.clip_in, f32[8,128]{1,0:T(8,128)} %get-tuple-element.7.reward_in), custom_call_target="tpu_custom_call" | custom-call | tf_op jit(solution)/shard_map/finish/pallas_call | solution.py:656

commit v5 on v4

--- a/solution.py
+++ b/solution.py
@@ -64,7 +64,7 @@
 
 def layer_back(whitened, inverse, scaled_grad):
     return inverse * (
-        scaled_grad - row_mean(scaled_grad) - whitened * row_mean(scaled_grad * whitened)
+        (scaled_grad - row_mean(scaled_grad)) - whitened * row_mean(scaled_grad * whitened)
     )
 
 
@@ -98,6 +98,17 @@
     copy.start()
     pending.append(copy)
     return copy
+
+
+def clip_partner(here, step):
+    return (
+        4 * lax.rem(here // 4 + step // 4, 2)
+        + 2 * lax.rem(here // 2 + step // 2, 2)
+        + lax.rem(here + step, 2)
+    )
+
+
+CLIP_STEPS = (6, 7, 4, 5, 2, 3, 1)
 
 
 def exchange(pick, slots, sems, here, place, count, pending):
@@ -147,6 +158,7 @@
     cols,
     first,
     slope,
+    lean,
     act,
     feat,
     embed,
@@ -160,6 +172,10 @@
     clip_out,
     reward_ref,
     back_cols,
+    swap,
+    to_patch,
+    from_patch,
+    own_channels,
     load_sem,
     conv_sem,
     patch_sem,
@@ -234,13 +250,13 @@
 
     mine = lat_seq.at[pl.ds(2 + local, 1)]
     copies = {}
-    for step in range(1, CLIP_DEV):
+    for step in CLIP_STEPS:
         copies[step] = start_copy(
             mine,
             mine,
             seq_sems.at[0, step],
             seq_sems.at[1, step],
-            in_clip(lax.rem(local + step, CLIP_DEV)),
+            in_clip(clip_partner(local, step)),
             pending,
         )
 
@@ -252,31 +268,10 @@
                 conv_ref.at[OUT_CH * near : OUT_CH * near + OUT_CH, CH * dt : CH * dt + CH],
                 conv_sem.at[dt, near],
             )
-    for k in range(4):
-        for s in range(SP):
-            load(
-                "patch",
-                patch_hbm.at[CH * k + OUT_CH * s : CH * k + OUT_CH * s + OUT_CH],
-                patch_ref.at[CH * s + OUT_CH * k : CH * s + OUT_CH * k + OUT_CH],
-                patch_sem.at[k, s],
-            )
-    load("qkv", qkv_hbm, qkv_ref, load_sem.at[7])
-    load("out", out_hbm, out_ref, load_sem.at[8])
-
-    wi_pad[27 * LAT :] = jnp.zeros((512 - 27 * LAT, CH), bf16)
-    lat_back[...] = jnp.zeros(lat_back.shape, f32)
-    placed[...] = jnp.zeros(placed.shape, f32)
     row, col = iota((512, 512), 0), iota((512, 512), 1)
-    swap = one_hot(
+    swap[...] = one_hot(
         ((row >> 7) == ((col >> 5) & 3)) & (((row >> 5) & 3) == (col >> 7)) & ((row & 31) == (col & 31))
     )
-    row, col = iota((256, 256), 0), iota((256, 256), 1)
-    kind, token = row >> 6, row & 63
-    to_patch = one_hot(
-        col == (2 * (token >> 4) + (kind & 1)) * ROWS + 2 * (token & 15) + (kind >> 1)
-    )
-    own_channels = one_hot(iota((CH, OUT_CH), 0) == iota((CH, OUT_CH), 1) + sp * OUT_CH)
-
     wait_all(copies)
 
     loaded("list")
@@ -293,9 +288,34 @@
             in_band(lax.rem(sp + step, SP)),
             pending,
         )
+
+    for k in range(4):
+        for s in range(SP):
+            load(
+                "patch",
+                patch_hbm.at[CH * k + OUT_CH * s : CH * k + OUT_CH * s + OUT_CH],
+                patch_ref.at[CH * s + OUT_CH * k : CH * s + OUT_CH * k + OUT_CH],
+                patch_sem.at[k, s],
+            )
+    load("qkv", qkv_hbm, qkv_ref, load_sem.at[7])
+    load("out", out_hbm, out_ref, load_sem.at[8])
+    wi_pad[27 * LAT :] = jnp.zeros((512 - 27 * LAT, CH), bf16)
+    lat_back[...] = jnp.zeros(lat_back.shape, f32)
+    placed[...] = jnp.zeros(placed.shape, f32)
+    row, col = iota((256, 256), 0), iota((256, 256), 1)
+
+    def cell_of(patch):
+        kind, token = patch >> 6, patch & 63
+        return (2 * (token >> 4) + (kind & 1)) * ROWS + 2 * (token & 15) + (kind >> 1)
+
+    to_patch[...] = one_hot(col == cell_of(row))
+    from_patch[...] = one_hot(row == cell_of(col))
+    own_channels[...] = one_hot(iota((CH, OUT_CH), 0) == iota((CH, OUT_CH), 1) + sp * OUT_CH)
+    loaded("gain", "wi", "conv")
     wait_all(copies)
+
     wide = jnp.concatenate([lat_sp[s] for s in range(SP)], axis=1)
-    spots = dot(wide, swap)
+    spots = dot(wide, swap[...])
     for c in range(3):
         for j in range(4):
             z_ref[2 * c + j // 2, 16 * (j % 2) : 16 * (j % 2) + 16] = spots[
@@ -331,7 +351,6 @@
 
     lax.fori_loop(0, COLS, build, 0, unroll=True)
 
-    loaded("gain", "wi")
     gain = gain_ref[...].reshape(1, CH)
     for frame in range(3):
         spots = dot(cols[frame].reshape(CELLS, 512), wi_pad[...])
@@ -344,9 +363,8 @@
             unit = h * lax.rsqrt(row_mean(h * h) + norm_epsilon) * gain
             act[rows, CH * frame : CH * frame + CH] = (unit * jax.nn.sigmoid(unit)).astype(bf16)
 
-    loaded("conv")
     spots = dot_last(act[...], conv_ref[...])
-    total = dot(first[2], own_channels).reshape(COLS, ROWS, OUT_CH)
+    total = dot(first[2], own_channels[...]).reshape(COLS, ROWS, OUT_CH)
     for dr in range(3):
         line = None
         for dc in range(3):
@@ -354,7 +372,7 @@
             term = moved(spots[:, start : start + OUT_CH].reshape(COLS, ROWS, OUT_CH), dc - 1)
             line = term if line is None else line + term
         total = total + shifted(line, dr - 1)
-    patches = dot(to_patch, total.reshape(CELLS, OUT_CH).astype(bf16))
+    patches = dot(to_patch[...], total.reshape(CELLS, OUT_CH).astype(bf16))
     feat[0] = jnp.concatenate(
         [patches[TOKENS * k : TOKENS * k + TOKENS] for k in range(4)], axis=1
     ).astype(bf16)
@@ -373,13 +391,14 @@
     for frame in range(3):
         h = first[frame].astype(f32)
         inverse = lax.rsqrt(row_mean(h * h) + norm_epsilon)
+        lean[frame] = h * (inverse * inverse)
         unit = h * inverse * gain
         gate = jax.nn.sigmoid(unit)
         slope[frame] = gate * (1.0 + unit * (1.0 - gate)) * (gain * inverse)
+    loaded("ln", "qkv", "out", "head", "scale")
     for step in (1, 3, 2):
         copies[step].wait_recv()
         embed_from(step)
-    loaded("ln", "qkv", "out", "head", "scale")
 
     x = embed[0]
     for s in range(1, SP):
@@ -422,13 +441,8 @@
     y = x + attended
     white_out, inverse_out = layer_stats(y)
     vector = head_ref[...].reshape(1, VW)
-    reward = jnp.sum(white_out * gain_out * vector, axis=1, keepdims=True)
-    reward_ref[...] = jnp.broadcast_to(
-        jnp.sum(reward, axis=0, keepdims=True) * (1.0 / TOKENS), (8, 128)
-    )
-    load("reward", reward_ref, reward_hbm, load_sem.at[9])
     scaled = (scale_ref[0] * (1.0 / TOKENS)) * vector * gain_out
-    dy = layer_back(white_out, inverse_out, jnp.broadcast_to(scaled, y.shape))
+    dy = layer_back(white_out, inverse_out, scaled)
     do = dot_last(dy.astype(bf16), out_ref[...]).astype(bf16)
     d_out = [do[:, HD * h : HD * h + HD] for h in heads]
     d_probs = jnp.concatenate([dot_last(d_out[h], value[h]) for h in heads], axis=0)
@@ -460,6 +474,12 @@
                 pending,
             )
 
+    reward = jnp.sum(white_out * gain_out * vector, axis=1, keepdims=True)
+    reward_ref[...] = jnp.broadcast_to(
+        jnp.sum(reward, axis=0, keepdims=True) * (1.0 / TOKENS), (8, 128)
+    )
+    load("reward", reward_ref, reward_hbm, load_sem.at[9])
+
     wait_all(copies)
 
     summed = patch_in[0].astype(f32)
@@ -468,7 +488,7 @@
     summed = jnp.concatenate(
         [summed[:, OUT_CH * k : OUT_CH * k + OUT_CH] for k in range(4)], axis=0
     )
-    d_feat = dot_first(to_patch, summed.astype(bf16))
+    d_feat = dot(from_patch[...], summed.astype(bf16))
     d_cells = d_feat.reshape(COLS, ROWS, OUT_CH)
     lines = [shifted(d_cells, 1 - dr).astype(bf16) for dr in range(3)]
     spread_out = jnp.concatenate(
@@ -479,14 +499,14 @@
         ],
         axis=1,
     )
-    d_own = dot_last(d_feat.astype(bf16), own_channels)
-
+    d_own = dot_last(d_feat.astype(bf16), own_channels[...])
+
+    d_acts = dot(spread_out, conv_ref[...])
     for frame in (2, 1, 0):
-        d_act = dot(spread_out, conv_ref[:, CH * frame : CH * frame + CH])
+        d_act = d_acts[:, CH * frame : CH * frame + CH]
         h = first[frame].astype(f32)
-        square = row_mean(h * h) + norm_epsilon
         d_unit = d_act * slope[frame]
-        d_first = d_unit - h * (row_mean(d_unit * h) / square)
+        d_first = d_unit - lean[frame] * row_mean(d_unit * h)
         if frame == 2:
             d_first = d_first + d_own
         back_cols[frame] = dot_last(d_first.astype(bf16), wi_pad[...]).reshape(COLS, ROWS, 512)
@@ -527,7 +547,7 @@
         ],
         axis=0,
     )
-    bands = dot(wide, swap).astype(bf16)
+    bands = dot(wide, swap[...]).astype(bf16)
     for s in range(SP):
         band_out[s] = bands[:, 128 * s : 128 * s + 128]
 
@@ -548,20 +568,24 @@
         summed = summed + band_in[s].astype(f32)
     placed[5:8] = summed.reshape(3, 16, 128)
     clip_out[...] = placed[pl.ds(7 - chunk, 8)].astype(bf16)
-    copies = exchange(
-        lambda step: clip_out.at[lax.rem(local + step, CLIP_DEV)],
-        clip_in,
-        clip_sems,
-        local,
-        in_clip,
-        CLIP_DEV,
-        pending,
-    )
+    copies = {}
+    for step in CLIP_STEPS:
+        peer = clip_partner(local, step)
+        copies[step] = start_copy(
+            clip_out.at[peer],
+            clip_in.at[step],
+            clip_sems.at[0, step],
+            clip_sems.at[1, step],
+            in_clip(peer),
+            pending,
+        )
     load("clip", clip_out.at[pl.ds(local, 1)], clip_in.at[0:1], load_sem.at[10])
+    loaded("clip", "reward")
+    for copy in pending[: 1 - CLIP_DEV]:
+        copy.wait_send()
     wait_all(copies)
 
-    loaded("clip", "reward")
-    for copy in pending:
+    for copy in pending[1 - CLIP_DEV :]:
         copy.wait_send()
 
 
@@ -616,6 +640,7 @@
             pltpu.VMEM((3, COLS, ROWS, 512), bf16),
             pltpu.VMEM((3, CELLS, CH), bf16),
             pltpu.VMEM((3, CELLS, CH), f32),
+            pltpu.VMEM((3, CELLS, CH), f32),
             pltpu.VMEM((CELLS, 3 * CH), bf16),
             pltpu.VMEM((SP, TOKENS, CH), bf16),
             pltpu.VMEM((SP, TOKENS, VW), f32),
@@ -629,6 +654,10 @@
             pltpu.VMEM((CLIP_DEV, 16, 128), bf16),
             pltpu.VMEM((8, 128), f32),
             pltpu.VMEM((3, COLS, ROWS, 512), f32),
+            pltpu.VMEM((512, 512), bf16),
+            pltpu.VMEM((CELLS, CELLS), bf16),
+            pltpu.VMEM((CELLS, CELLS), bf16),
+            pltpu.VMEM((CH, OUT_CH), bf16),
             pltpu.SemaphoreType.DMA((11,)),
             pltpu.SemaphoreType.DMA((3, 9)),
             pltpu.SemaphoreType.DMA((4, SP)),

time: 49.7 us -> 48.9 us (0.984)
  Pallas kernels: 48.2 us -> 47.4 us
    pallas_call x1, Pallas kernels: 46.8 us -> 45.9 us  [body(): pl.pallas_call(kernel, out_shape=(jax.ShapeDtypeStruct((CLIP_DEV, 16, 128...]
where the time goes in v5:
time: 48.9 us; the launch traced here: 48.7 us
  Pallas kernels  47.4 us (97%)
  between operations  1.29 us (3%)
    pallas_call x1, Pallas kernels, body(): pl.pallas_call(kernel, out_shape=(jax.ShapeDtypeStruct((CLIP_DEV, 16, 128...  45.9 us
    pallas_call x1, Pallas kernels, body(): pl.pallas_call(finish, out_shape=(jax.ShapeDtypeStruct((1, 1), f32), jax....  1.46 us

profile of v5, /device:TPU:1, one launch (start us, length us, event | category | flops | bytes accessed | tf_op | source)
XLA Modules:
  0.0 48.7 jit_solution(105433470892183907)
XLA Ops:
  1.3 45.9 %reward_step.1 = (bf16[8,16,128]{2,1,0:T(8,128)(2,1)}, f32[8,128]{1,0:T(8,128)}) custom-call(bf16[2,32,32]{2,1,0:T(8,128)(2,1)} %lat_hbm.1, s32[64]{0:T(128)} %list_hbm.1, f32[1]{0:T(128)S(6)} %copy.13.scale_hbm, f32[384]{0:T(512)} %gain_hbm.1, bf16[432,384]{1,0:T(8,128)(2,1)} %wi_hbm.1, f32[2,1024]{1,0:T(2,128)} %ln_hbm.1, f32[1024]{0:T(1024)} %head_hbm.1, ...), custom_call_target="tpu_custom_call" | custom-call | tf_op jit(solution)/shard_map/reward_step/pallas_call | solution.py:616
  47.2 1.5 %finish.1 = (f32[1,1]{1,0:T(1,128)}, f32[2,32,32]{2,1,0:T(8,128)}) custom-call(bf16[8,16,128]{2,1,0:T(8,128)(2,1)} %get-tuple-element.6.clip_in, f32[8,128]{1,0:T(8,128)} %get-tuple-element.7.reward_in), custom_call_target="tpu_custom_call" | custom-call | tf_op jit(solution)/shard_map/finish/pallas_call | solution.py:685

commit v6 on v5

--- a/solution.py
+++ b/solution.py
@@ -109,6 +109,10 @@
 
 
 CLIP_STEPS = (6, 7, 4, 5, 2, 3, 1)
+ALL_STEPS = sorted(
+    ((clip, band) for clip in range(CLIP_DEV) for band in range(SP) if clip or band),
+    key=lambda step: -((0, 0, 1, 1, 2, 2, 2, 2)[step[0]] + (0, 1, 2, 1)[step[1]]),
+)
 
 
 def exchange(pick, slots, sems, here, place, count, pending):
@@ -166,8 +170,6 @@
     patch_out,
     patch_in,
     lat_back,
-    band_out,
-    band_in,
     placed,
     clip_out,
     reward_ref,
@@ -185,7 +187,6 @@
     feat_sems,
     mix_sems,
     patch_sems,
-    band_sems,
 ):
     seq = lax.axis_index("seq")
     sp = lax.axis_index("sp")
@@ -301,7 +302,7 @@
     load("out", out_hbm, out_ref, load_sem.at[8])
     wi_pad[27 * LAT :] = jnp.zeros((512 - 27 * LAT, CH), bf16)
     lat_back[...] = jnp.zeros(lat_back.shape, f32)
-    placed[...] = jnp.zeros(placed.shape, f32)
+    placed[...] = jnp.zeros(placed.shape, bf16)
     row, col = iota((256, 256), 0), iota((256, 256), 1)
 
     def cell_of(patch):
@@ -548,50 +549,36 @@
         axis=0,
     )
     bands = dot(wide, swap[...]).astype(bf16)
+    placed[5:8] = bands.reshape(3, 16, 512)
+    ready = placed[pl.ds(7 - chunk, 8)]
     for s in range(SP):
-        band_out[s] = bands[:, 128 * s : 128 * s + 128]
-
-    copies = exchange(
-        lambda step: band_out.at[lax.rem(sp + step, SP)],
-        band_in,
-        band_sems,
-        sp,
-        in_band,
-        SP,
-        pending,
-    )
-    band_in[pl.ds(0, 1)] = band_out[pl.ds(sp, 1)]
-    wait_all(copies)
-
-    summed = band_in[0].astype(f32)
-    for s in range(1, SP):
-        summed = summed + band_in[s].astype(f32)
-    placed[5:8] = summed.reshape(3, 16, 128)
-    clip_out[...] = placed[pl.ds(7 - chunk, 8)].astype(bf16)
+        clip_out[s] = ready[:, :, 128 * s : 128 * s + 128]
+
     copies = {}
-    for step in CLIP_STEPS:
-        peer = clip_partner(local, step)
-        copies[step] = start_copy(
-            clip_out.at[peer],
-            clip_in.at[step],
-            clip_sems.at[0, step],
-            clip_sems.at[1, step],
-            in_clip(peer),
+    for clip_step, band_step in ALL_STEPS:
+        slot = SP * clip_step + band_step
+        peer, band = clip_partner(local, clip_step), lax.rem(sp + band_step, SP)
+        copies[slot] = start_copy(
+            clip_out.at[band, peer],
+            clip_in.at[slot],
+            clip_sems.at[0, slot],
+            clip_sems.at[1, slot],
+            (base + peer, band),
             pending,
         )
-    load("clip", clip_out.at[pl.ds(local, 1)], clip_in.at[0:1], load_sem.at[10])
+    load("clip", clip_out.at[sp, local], clip_in.at[0], load_sem.at[10])
     loaded("clip", "reward")
-    for copy in pending[: 1 - CLIP_DEV]:
+    for copy in pending[: 1 - CLIP_DEV * SP]:
         copy.wait_send()
     wait_all(copies)
 
-    for copy in pending[1 - CLIP_DEV :]:
+    for copy in pending[1 - CLIP_DEV * SP :]:
         copy.wait_send()
 
 
 def finish(clip_in, reward_in, reward_ref, grad_ref):
     summed = clip_in[0].astype(f32)
-    for s in range(1, CLIP_DEV):
+    for s in range(1, CLIP_DEV * SP):
         summed = summed + clip_in[s].astype(f32)
     for j in range(4):
         grad_ref[j // 2, 16 * (j % 2) : 16 * (j % 2) + 16] = summed[:, 32 * j : 32 * j + 32]
@@ -616,7 +603,7 @@
     parts, rewards = pl.pallas_call(
         kernel,
         out_shape=(
-            jax.ShapeDtypeStruct((CLIP_DEV, 16, 128), bf16),
+            jax.ShapeDtypeStruct((CLIP_DEV * SP, 16, 128), bf16),
             jax.ShapeDtypeStruct((8, 128), f32),
         ),
         in_specs=[hbm] * 11,
@@ -648,10 +635,8 @@
             pltpu.VMEM((SP, TOKENS, CH), bf16),
             pltpu.VMEM((SP, TOKENS, CH), bf16),
             pltpu.VMEM((7, ROWS, 128), f32),
-            pltpu.VMEM((SP, 48, 128), bf16),
-            pltpu.VMEM((SP, 48, 128), bf16),
-            pltpu.VMEM((15, 16, 128), f32),
-            pltpu.VMEM((CLIP_DEV, 16, 128), bf16),
+            pltpu.VMEM((15, 16, 512), bf16),
+            pltpu.VMEM((SP, CLIP_DEV, 16, 128), bf16),
             pltpu.VMEM((8, 128), f32),
             pltpu.VMEM((3, COLS, ROWS, 512), f32),
             pltpu.VMEM((512, 512), bf16),
@@ -662,9 +647,9 @@
             pltpu.SemaphoreType.DMA((3, 9)),
             pltpu.SemaphoreType.DMA((4, SP)),
             pltpu.SemaphoreType.DMA((2, CLIP_DEV)),
-            pltpu.SemaphoreType.DMA((2, CLIP_DEV)),
+            pltpu.SemaphoreType.DMA((2, CLIP_DEV * SP)),
         ]
-        + [pltpu.SemaphoreType.DMA((2, SP))] * 5,
+        + [pltpu.SemaphoreType.DMA((2, SP))] * 4,
         compiler_params=pltpu.CompilerParams(
             collective_id=0, has_side_effects=True, vmem_limit_bytes=60 * 1024 * 1024
         ),

time: 48.9 us -> 47.5 us (0.971)
  Pallas kernels: 47.4 us -> 46.1 us
    pallas_call x1, Pallas kernels: 45.9 us -> 44.4 us  [body(): pl.pallas_call(kernel, out_shape=(jax.ShapeDtypeStruct((CLIP_DEV * SP, 16...]
where the time goes in v6:
time: 47.5 us; the launch traced here: 47.3 us
  Pallas kernels  46.1 us (97%)
  between operations  1.29 us (3%)
    pallas_call x1, Pallas kernels, body(): pl.pallas_call(kernel, out_shape=(jax.ShapeDtypeStruct((CLIP_DEV * SP, 16...  44.4 us
    pallas_call x1, Pallas kernels, body(): pl.pallas_call(finish, out_shape=(jax.ShapeDtypeStruct((1, 1), f32), jax....  1.63 us

profile of v6, /device:TPU:1, one launch (start us, length us, event | category | flops | bytes accessed | tf_op | source)
XLA Modules:
  0.0 47.3 jit_solution(6672194224030506226)
XLA Ops:
  1.3 44.4 %reward_step.1 = (bf16[32,16,128]{2,1,0:T(8,128)(2,1)}, f32[8,128]{1,0:T(8,128)}) custom-call(bf16[2,32,32]{2,1,0:T(8,128)(2,1)} %lat_hbm.1, s32[64]{0:T(128)} %list_hbm.1, f32[1]{0:T(128)S(6)} %copy.13.scale_hbm, f32[384]{0:T(512)} %gain_hbm.1, bf16[432,384]{1,0:T(8,128)(2,1)} %wi_hbm.1, f32[2,1024]{1,0:T(2,128)} %ln_hbm.1, f32[1024]{0:T(1024)} %head_hbm.1, ...), custom_call_target="tpu_custom_call" | custom-call | tf_op jit(solution)/shard_map/reward_step/pallas_call | solution.py:603
  45.7 1.6 %finish.1 = (f32[1,1]{1,0:T(1,128)}, f32[2,32,32]{2,1,0:T(8,128)}) custom-call(bf16[32,16,128]{2,1,0:T(8,128)(2,1)} %get-tuple-element.6.clip_in, f32[8,128]{1,0:T(8,128)} %get-tuple-element.7.reward_in), custom_call_target="tpu_custom_call" | custom-call | tf_op jit(solution)/shard_map/finish/pallas_call | solution.py:670

commit v7 on v6

--- a/solution.py
+++ b/solution.py
@@ -273,11 +273,11 @@
     swap[...] = one_hot(
         ((row >> 7) == ((col >> 5) & 3)) & (((row >> 5) & 3) == (col >> 7)) & ((row & 31) == (col & 31))
     )
-    wait_all(copies)
-
     loaded("list")
     where = lax.rem(list_ref[seq], CLIP_FR)
     chunk, odd = lax.div(where, 2), lax.rem(where, 2)
+    wait_all(copies)
+
     lat_sp[pl.ds(sp, 1)] = lat_seq[pl.ds(chunk, 3)].reshape(1, 48, 128)
     copies = {}
     for step in (2, 1, 3):
@@ -419,7 +419,7 @@
     query, key, value = part_of(0), part_of(1), part_of(2)
     scores = jnp.concatenate([dot_last(query[h], key[h]) for h in heads], axis=0) * (HD**-0.5)
     weights = jnp.exp(scores - jnp.max(scores, axis=-1, keepdims=True))
-    probs = weights / jnp.sum(weights, axis=-1, keepdims=True)
+    probs = weights * (1.0 / jnp.sum(weights, axis=-1, keepdims=True))
     probs_low = rows_of(probs.astype(bf16))
     mixed = [dot(probs_low[h], value[h]).astype(bf16) for h in heads]
     mix[pl.ds(sp, 1)] = dot(jnp.concatenate(mixed, axis=1), out_ref[...]).astype(bf16)[None]
@@ -481,11 +481,11 @@
     )
     load("reward", reward_ref, reward_hbm, load_sem.at[9])
 
-    wait_all(copies)
-
     summed = patch_in[0].astype(f32)
-    for s in range(1, SP):
-        summed = summed + patch_in[s].astype(f32)
+    for step in (1, 3, 2):
+        copies[step].wait_recv()
+        summed = summed + patch_in[step].astype(f32)
+
     summed = jnp.concatenate(
         [summed[:, OUT_CH * k : OUT_CH * k + OUT_CH] for k in range(4)], axis=0
     )

time: 47.5 us -> 47.5 us (level)
  no operation moved by 1% of the time
where the time goes in v7:
time: 47.5 us; the launch traced here: 47.3 us
  Pallas kernels  46.1 us (97%)
  between operations  1.29 us (3%)
    pallas_call x1, Pallas kernels, body(): pl.pallas_call(kernel, out_shape=(jax.ShapeDtypeStruct((CLIP_DEV * SP, 16...  44.4 us
    pallas_call x1, Pallas kernels, body(): pl.pallas_call(finish, out_shape=(jax.ShapeDtypeStruct((1, 1), f32), jax....  1.63 us

profile of v7, /device:TPU:1, one launch (start us, length us, event | category | flops | bytes accessed | tf_op | source)
XLA Modules:
  0.0 47.3 jit_solution(13485654725865516550)
XLA Ops:
  1.3 44.4 %reward_step.1 = (bf16[32,16,128]{2,1,0:T(8,128)(2,1)}, f32[8,128]{1,0:T(8,128)}) custom-call(bf16[2,32,32]{2,1,0:T(8,128)(2,1)} %lat_hbm.1, s32[64]{0:T(128)} %list_hbm.1, f32[1]{0:T(128)S(6)} %copy.13.scale_hbm, f32[384]{0:T(512)} %gain_hbm.1, bf16[432,384]{1,0:T(8,128)(2,1)} %wi_hbm.1, f32[2,1024]{1,0:T(2,128)} %ln_hbm.1, f32[1024]{0:T(1024)} %head_hbm.1, ...), custom_call_target="tpu_custom_call" | custom-call | tf_op jit(solution)/shard_map/reward_step/pallas_call | solution.py:603
  45.7 1.6 %finish.1 = (f32[1,1]{1,0:T(1,128)}, f32[2,32,32]{2,1,0:T(8,128)}) custom-call(bf16[32,16,128]{2,1,0:T(8,128)(2,1)} %get-tuple-element.6.clip_in, f32[8,128]{1,0:T(8,128)} %get-tuple-element.7.reward_in), custom_call_target="tpu_custom_call" | custom-call | tf_op jit(solution)/shard_map/finish/pallas_call | solution.py:670
